TPU v7x, 256 devices: a whole 4x4x8 slice. The times are simulated.
256 devices in a mesh: dp: 32 (over y, z), hidden: 8 (over x, core).
Axes of the slice: x: 4, y: 4, z: 8, core: 2. Of those that a mesh axis runs over, the one named last changes fastest.
Arguments:
- tokens: bfloat16 [4096, 4096], P('dp'), may hold values from -6 to 6
- gate_weight: bfloat16 [4096, 14336], P('dp', 'hidden'), may hold values from -0.09375 to 0.09375
- up_weight: bfloat16 [4096, 14336], P('dp', 'hidden'), may hold values from -0.09375 to 0.09375
- cotangent: bfloat16 [4096, 4096], P('dp'), may hold values from -6 to 6
- query_left: bfloat16 [512, 14336], P(None, 'hidden'), may hold values from -0.046875 to 0.046875
- query_right: bfloat16 [512, 4096], P('hidden'), may hold values from -0.005859375 to 0.005859375
- doc_ids: int32 [4096], P('dp'), may hold values from 0 to 255, never falling along the last dimension, each value on 1 to 256 neighbouring positions
- doc_slot: int32 [256], replicated, may hold values from 0 to 255, each once
Outputs:
- doc_scores: float32 [16, 256], P('hidden', 'dp')
Inputs may be any that keep to these rules, and one draw needn't show every extreme that they name: `doc_ids`: document numbers never fall along the 4096 tokens; every document has 1 to 256 tokens and one has exactly 256. `doc_slot`: each column is named by exactly one document.
All inputs are finite; a program needn't handle non-finite values.
Results may differ from a plain program's by a relative error of at most 0.0031.
Values may be sent and summed in bfloat16 or wider, within the bound.
A program may use at most 128 MiB of HBM per device.

v0:
```python
import jax
import jax.numpy as jnp
from jax import lax
from jax.sharding import PartitionSpec as P

R = 32


def add_rows(window, weight_piece):
    return jnp.dot(window, weight_piece, preferred_element_type=jnp.float32)


def local(tokens, gate_weight, up_weight, cotangent, query_left, query_right, doc_ids, doc_slot):
    contract_dims = (((1,), (1,)), ((), ()))

    def add_single(weight_piece):
        return add_rows(tokens, weight_piece)

    gate = add_single(lax.all_gather(gate_weight, "dp", axis=0, tiled=True))
    up_part = add_single(lax.all_gather(up_weight, "dp", axis=0, tiled=True))
    hidden_act = (jax.nn.silu(gate) * up_part).astype(jnp.bfloat16)
    right_proj = lax.dot_general(
        query_right, cotangent, contract_dims, preferred_element_type=jnp.float32
    )
    row_count = query_right.shape[0]
    partial_proj = lax.dot_general(
        query_left, hidden_act, contract_dims, preferred_element_type=jnp.float32
    )
    summed = lax.psum(partial_proj, "hidden")
    left_proj = lax.dynamic_slice_in_dim(summed, lax.axis_index("hidden") * row_count, row_count, 0)
    token_scores = (left_proj * right_proj).reshape(row_count // R, R, tokens.shape[0]).sum(axis=1)
    doc_count = doc_slot.shape[0]
    doc_range = jnp.arange(doc_count, dtype=jnp.int32)
    one_hot = (doc_ids[:, None] == doc_range[None, :]).astype(jnp.float32)
    by_doc = jnp.dot(token_scores, one_hot, precision=lax.Precision.HIGHEST)
    placing = (doc_slot[:, None] == doc_range[None, :]).astype(jnp.float32)
    by_column = jnp.dot(by_doc, placing, precision=lax.Precision.HIGHEST)
    return lax.psum_scatter(by_column, "dp", scatter_dimension=1, tiled=True)


def solution(mesh):
    return jax.shard_map(
        local,
        mesh=mesh,
        in_specs=(
            P("dp", None),
            P("dp", "hidden"),
            P("dp", "hidden"),
            P("dp", None),
            P(None, "hidden"),
            P("hidden", None),
            P("dp"),
            P(),
        ),
        out_specs=P("hidden", "dp"),
        check_vma=False,
    )
```

profile of v0, /device:TPU:0, one launch (start us, length us, event | category | flops | bytes accessed | tf_op | source)
XLA Modules:
  0.0 426.4 jit_solution(1485521692856060211)
XLA Ops:
  6.5 0.0 copy-start
  6.5 0.0 copy-start.1
  6.5 0.0 all-gather.3.cloned.1.call-start
  6.5 0.7 all-gather.3.cloned.1.call-update
  7.3 0.0 all-gather.5.cloned.1.call-start
  7.3 0.7 all-gather.5.cloned.1.call-update
  8.0 0.0 all-reduce.3.cloned.1.call-start
  8.1 133.2 %all-gather.3.cloned.1.call-done = bf16[4096,1792]{1,0:T(8,128)(2,1)} async-done(((bf16[128,1792]{1,0:T(8,128)(2,1)}), bf16[4096,1792]{1,0:T(8,128)(2,1)}) %all-gather.3.cloned.1.call-update) | async-done | bytes 14680080 | tf_op jit(solution)/shard_map/all_gather | solution.py:19
  141.3 8.6 %fusion.12 = f32[128,1792]{1,0:T(8,128)} fusion(bf16[128,4096]{1,0:T(8,128)(2,1)} %param.8, bf16[4096,1792]{1,0:T(8,128)(2,1)} %all-gather.3.cloned.1.call-done), kind=kOutput, calls=%fused_computation.19 | convolution fusion | flops 1879048192 | bytes 16646144 | tf_op jit(solution)/shard_map/dot_general | solution.py:10
  149.8 0.0 copy-start.5
  149.8 0.0 copy-start.2
  149.8 0.0 copy-start.4
  149.8 0.0 copy-start.3
  149.8 121.1 %all-gather.5.cloned.1.call-done = bf16[4096,1792]{1,0:T(8,128)(2,1)} async-done(((bf16[128,1792]{1,0:T(8,128)(2,1)}), bf16[4096,1792]{1,0:T(8,128)(2,1)}) %all-gather.5.cloned.1.call-update) | async-done | bytes 14680080 | tf_op jit(solution)/shard_map/all_gather | solution.py:20
  271.0 0.0 copy-done
  271.0 0.0 copy-done.1
  271.0 8.8 %convolution_bitcast_fusion = f32[512,128]{1,0:T(8,128)} fusion(bf16[512,1792]{1,0:T(8,128)(2,1)S(1)} %copy-done, bf16[128,4096]{1,0:T(8,128)(2,1)S(1)} %copy-done.1, bf16[4096,1792]{1,0:T(8,128)(2,1)} %all-gather.5.cloned.1.call-done, f32[128,1792]{1,0:T(8,128)} %fusion.12), kind=kOutput, calls=%fused_computation.2 | convolution fusion | flops 2115305472 | bytes 18743296 | tf_op jit(solution)/shard_map/dot_general | solution.py:26
  279.8 0.0 all-reduce.3.cloned.1.call-update
  279.8 0.0 copy-done.5
  279.8 0.6 dynamic-slice
  281.1 60.8 %all-reduce.3.cloned.1.call-done = f32[512,128]{1,0:T(8,128)} async-done(((f32[512,128]{1,0:T(8,128)}), f32[512,128]{1,0:T(8,128)}) %all-reduce.3.cloned.1.call-update) | async-done | bytes 262160 | tf_op jit(solution)/shard_map/psum | solution.py:29
  341.9 0.0 copy-done.2
  341.9 1.7 bitcast_reduce_fusion
  343.6 0.0 copy-done.4
  343.6 0.2 fusion.9
  343.8 0.0 copy-done.3
  343.8 0.2 fusion.7
  344.1 75.1 %all-reduce = f32[2,256]{1,0:T(2,128)S(1)} all-reduce(f32[2,256]{1,0:T(2,128)S(1)} %fusion.7), channel_id=2, replica_groups=mesh['dp'=32,'hidden'=8] {'dp'}, use_global_device_ids=true, to_apply=%region_2.3.clone | all-reduce | flops 512 | bytes 4096
  419.2 0.6 constant_dynamic-slice_fusion
Async XLA Ops:
  6.5 264.4 %copy-start = (bf16[512,1792]{1,0:T(8,128)(2,1)S(1)}, bf16[512,1792]{1,0:T(8,128)(2,1)}, u32[]{:S(2)}) copy-start(bf16[512,1792]{1,0:T(8,128)(2,1)} %param.12) | copy-start | bytes 5505028
  6.5 264.4 %copy-start.1 = (bf16[128,4096]{1,0:T(8,128)(2,1)S(1)}, bf16[128,4096]{1,0:T(8,128)(2,1)}, u32[]{:S(2)}) copy-start(bf16[128,4096]{1,0:T(8,128)(2,1)} %param.8) | copy-start | bytes 3145732
  6.5 134.7 %all-gather.3.cloned.1.call-start = ((), (), s32[]{:S(2)}) async-start(), calls=%async_computation | async-start | bytes 15138816 | tf_op jit(solution)/shard_map/all_gather | solution.py:19
  7.3 263.7 %all-gather.5.cloned.1.call-start = ((), (), s32[]{:S(2)}) async-start(), calls=%async_computation.1 | async-start | bytes 15138816 | tf_op jit(solution)/shard_map/all_gather | solution.py:20
  8.0 333.9 %all-reduce.3.cloned.1.call-start = ((), (), s32[]{:S(2)}) async-start(), calls=%async_computation.2 | async-start | bytes 524288 | tf_op jit(solution)/shard_map/psum | solution.py:29
  149.8 130.0 %copy-start.5 = (u32[256]{0:T(256)S(1)}, u32[256]{0:T(256)}, u32[]{:S(2)}) copy-start(u32[256]{0:T(256)} %constant.17) | copy-start | bytes 3076
  149.8 192.1 %copy-start.2 = (bf16[64,4096]{1,0:T(8,128)(2,1)S(1)}, bf16[64,4096]{1,0:T(8,128)(2,1)}, u32[]{:S(2)}) copy-start(bf16[64,4096]{1,0:T(8,128)(2,1)} %param.13) | copy-start | bytes 1572868
  149.8 193.8 %copy-start.4 = (s32[128]{0:T(128)S(1)}, s32[128]{0:T(128)}, u32[]{:S(2)}) copy-start(s32[128]{0:T(128)} %param.14) | copy-start | bytes 1540
  149.8 194.0 %copy-start.3 = (s32[256]{0:T(256)S(1)}, s32[256]{0:T(256)}, u32[]{:S(2)}) copy-start(s32[256]{0:T(256)} %param.15) | copy-start | bytes 3076
Sparse Core Ops, SparseCore 0:
  9.9 131.2 all-gather.2
  143.8 127.1 all-gather.4
  279.9 61.9 all-reduce.2
where the time goes:
time: 427 us; the launch traced here: 426 us
  waiting for transfers between devices  317 us (74%)
  blocking collectives  75.1 us (18%)
  matrix products  19.6 us (5%)
  between operations  13.8 us (3%)
    all_gather x1, waiting for transfers between devices, local(): gate = add_single(lax.all_gather(gate_weight, 'dp', axis=0, tiled=True))  133 us
    all_gather x1, waiting for transfers between devices, local(): up_part = add_single(lax.all_gather(up_weight, 'dp', axis=0, tiled=True))  121 us
    unnamed x1, blocking collectives  75.1 us
    psum x1, waiting for transfers between devices, local(): summed = lax.psum(partial_proj, 'hidden')  60.8 us
    dot_general x1, matrix products, local(): lax.dot_general(query_left, hidden_act, contract_dims, preferred_element_...  8.81 us
    dot_general x1, matrix products, add_rows(): return jnp.dot(window, weight_piece, preferred_element_type=jnp.float32)  8.58 us
  transfers between devices with their start and end apart: 3, of which 3 were waited for; matrix products, arithmetic and copies ran while one was open for 2% of the time, Pallas kernels for 0%

commit v1 on v0

v1 whole, which is shorter than its diff:
```python
import jax
import jax.numpy as jnp
from jax import lax
from jax.sharding import PartitionSpec as P

R = 32
NY, NZ = 4, 8
Z_GROUPS = [[y * NZ + z for z in range(NZ)] for y in range(NY)]
Y_GROUPS = [[y * NZ + z for y in range(NY)] for z in range(NZ)]


def local(tokens, gate_weight, up_weight, cotangent, query_left, query_right, doc_ids, doc_slot):
    contract_last = (((1,), (1,)), ((), ()))
    hidden = lax.axis_index("hidden")
    z = lax.rem(lax.axis_index("dp"), NZ)
    rows, units = gate_weight.shape
    part = units // NZ
    both = jnp.stack([gate_weight.T, up_weight.T]).reshape(2, NZ, part, rows)
    mixed = lax.all_to_all(both, "dp", 1, 1, axis_index_groups=Z_GROUPS, tiled=True)
    weights = lax.all_gather(mixed, "dp", axis=0, axis_index_groups=Y_GROUPS)
    weights = weights.transpose(1, 3, 0, 2, 4).reshape(2 * part, NY * NZ * rows)

    count = tokens.shape[0] // 8
    piece = lax.dynamic_slice_in_dim(tokens, hidden * count, count, 0)
    pieces = lax.all_gather(piece, "dp", axis=0, axis_index_groups=Z_GROUPS)
    window = lax.all_gather(pieces, "hidden", axis=1).reshape(NZ * tokens.shape[0], -1)

    pre = lax.dot_general(weights, window, contract_last, preferred_element_type=jnp.float32)
    hidden_act = (jax.nn.silu(pre[:part]) * pre[part:]).astype(jnp.bfloat16)
    left = lax.dynamic_slice_in_dim(query_left, z * part, part, 1)
    partial_proj = jnp.dot(left, hidden_act, preferred_element_type=jnp.float32)

    right = lax.dot_general(query_right, cotangent, contract_last, preferred_element_type=jnp.float32)
    right = lax.all_gather(right, "hidden", axis=0, tiled=True)
    right = lax.all_gather(right, "dp", axis=1, axis_index_groups=Z_GROUPS, tiled=True)
    ids = lax.all_gather(doc_ids, "dp", axis=0, axis_index_groups=Z_GROUPS, tiled=True)
    queries = partial_proj.shape[0] // R
    token_scores = (partial_proj * right).reshape(queries, R, -1).sum(axis=1)
    doc_range = jnp.arange(doc_slot.shape[0], dtype=jnp.int32)
    one_hot = (ids[:, None] == doc_range[None, :]).astype(jnp.float32)
    by_doc = jnp.dot(token_scores, one_hot, precision=lax.Precision.HIGHEST)
    placing = (doc_slot[:, None] == doc_range[None, :]).astype(jnp.float32)
    by_column = jnp.dot(by_doc, placing, precision=lax.Precision.HIGHEST)
    mine = lax.psum_scatter(by_column, "hidden", scatter_dimension=0, tiled=True)
    return lax.psum_scatter(mine, "dp", scatter_dimension=1, tiled=True)


def solution(mesh):
    return jax.shard_map(
        local,
        mesh=mesh,
        in_specs=(
            P("dp", None),
            P("dp", "hidden"),
            P("dp", "hidden"),
            P("dp", None),
            P(None, "hidden"),
            P("hidden", None),
            P("dp"),
            P(),
        ),
        out_specs=P("hidden", "dp"),
        check_vma=False,
    )
```

time: 427 us -> 316 us (0.74)
  waiting for transfers between devices: 317 us -> 103 us
  blocking collectives: 75.1 us -> 165 us
  local copies, waits for them, and re-layouts: 1.24 us -> 19.2 us
  matrix products: 19.6 us -> 13.8 us
    all_gather x2 -> x4, waiting for transfers between devices: 254 us -> 103 us  [the longest x1 42.4 us: local(): lax.all_gather(pieces, 'hidden', axis=1).reshape(NZ * tokens.shape[0], -1)]
    psum x1 -> x0, waiting for transfers between devices: 60.8 us -> none  [local(): summed = lax.psum(partial_proj, 'hidden')]
    all_to_all x0 -> x1, blocking collectives: none -> 39 us  [local(): lax.all_to_all(both, 'dp', 1, 1, axis_index_groups=Z_GROUPS, tiled=True)]
    all_gather x0 -> x2, blocking collectives: none -> 28.6 us  [the longest x1 14.8 us: local(): right = lax.all_gather(right, 'hidden', axis=0, tiled=True)]
    unnamed x1 -> x2, blocking collectives: 75.1 us -> 97.7 us
    reshape x0 -> x1, local copies, waits for them, and re-layouts: none -> 6.67 us  [local(): weights = weights.transpose(1, 3, 0, 2, 4).reshape(2 * part, NY * NZ * rows)]
    dot_general x3, matrix products: 19.1 us -> 13.1 us  [the longest x1 9.8 us: local(): lax.dot_general(weights, window, contract_last, preferred_element_type=jn...]
    all_gather x0 -> x1, local copies, waits for them, and re-layouts: none -> 5.28 us  [local(): weights = lax.all_gather(mixed, 'dp', axis=0, axis_index_groups=Y_GROUPS)]
  transfers between devices with their start and end apart: 3 -> 4, of which waited for: 3 -> 4; matrix products, arithmetic and copies ran while one was open for 2% -> 9% of each run, Pallas kernels for 0% -> 0%
where the time goes in v1:
time: 316 us
  blocking collectives  165 us (52%)
  waiting for transfers between devices  103 us (33%)
  local copies, waits for them, and re-layouts  19.2 us (6%)
  between operations  14.5 us (5%)
  matrix products  13.8 us (4%)
    unnamed x2, blocking collectives  97.7 us
    all_gather x1, waiting for transfers between devices, local(): lax.all_gather(pieces, 'hidden', axis=1).reshape(NZ * tokens.shape[0], -1)  42.4 us
    all_gather x1, waiting for transfers between devices, local(): lax.all_gather(right, 'dp', axis=1, axis_index_groups=Z_GROUPS, tiled=True)  39.8 us
    all_to_all x1, blocking collectives, local(): lax.all_to_all(both, 'dp', 1, 1, axis_index_groups=Z_GROUPS, tiled=True)  39 us
    all_gather x1, waiting for transfers between devices, local(): weights = lax.all_gather(mixed, 'dp', axis=0, axis_index_groups=Y_GROUPS)  15 us
    all_gather x1, blocking collectives, local(): right = lax.all_gather(right, 'hidden', axis=0, tiled=True)  14.8 us
    all_gather x1, blocking collectives, local(): lax.all_gather(doc_ids, 'dp', axis=0, axis_index_groups=Z_GROUPS, tiled=T...  13.8 us
    dot_general x1, matrix products, local(): lax.dot_general(weights, window, contract_last, preferred_element_type=jn...  9.8 us
  transfers between devices with their start and end apart: 4, of which 4 were waited for; matrix products, arithmetic and copies ran while one was open for 9% of the time, Pallas kernels for 0%

profile of v1, /device:TPU:0, one launch (start us, length us, event | category | flops | bytes accessed | tf_op | source)
XLA Modules:
  0.0 315.5 jit_solution(4047472257433530554)
XLA Ops:
  6.5 1.7 constant_dynamic-slice_fusion.2
  8.2 0.0 all-gather.13.cloned.1.call-update
  8.3 0.0 all-gather.11.cloned.1.call-start
  8.3 1.3 copy.12
  9.6 1.3 copy.13
  10.9 0.1 pad_maximum_fusion
  11.0 0.1 copy.14
  11.0 39.0 %all_to_all.5 = bf16[2,8,224,128]{3,2,0,1:T(8,128)(2,1)S(1)} all-to-all(bf16[2,8,224,128]{3,2,0,1:T(8,128)(2,1)S(1)} %copy.14), channel_id=1, replica_groups={{0,8,16,24,32,40,48,56},{64,72,80,88,96,104,112,120},{128,136,144,152,1..., dimensions={1} | all-to-all | bytes 1835008 | tf_op jit(solution)/shard_map/all_to_all | solution.py:19
  50.0 1.0 copy.15
  51.0 0.0 all-gather.11.cloned.1.call-update
  51.1 0.0 all-gather.15.cloned.1.call-start
  51.1 5.2 %all-gather.13.cloned.1.call-done = bf16[128,4096]{1,0:T(8,128)(2,1)} async-done(((bf16[16,4096]{1,0:T(8,128)(2,1)}), bf16[128,4096]{1,0:T(8,128)(2,1)}) %all-gather.13.cloned.1.call-update) | async-done | bytes 1048592 | tf_op jit(solution)/shard_map/all_gather | solution.py:25
  56.3 0.0 all-gather.15.cloned.1.call-update
  56.4 0.0 all-gather.9.cloned.1.call-start
  56.4 0.5 fusion.11
  56.9 14.8 %all_gather.33 = f32[512,128]{1,0:T(8,128)} all-gather(f32[64,128]{1,0:T(8,128)S(1)} %fusion.11), channel_id=1, replica_groups=mesh['dp'=32,'hidden'=8] {'hidden'}, dimensions={0}, use_global_device_ids=true | all-gather | bytes 294912 | tf_op jit(solution)/shard_map/all_gather | solution.py:34
  71.7 0.0 all-gather.9.cloned.1.call-update
  71.7 0.6 dynamic-slice
  72.3 0.6 dynamic-slice.2
  74.3 13.8 %all-gather.3 = s32[8,1,128]{2,1,0:T(1,128)S(1)} all-gather(s32[1,1,128]{2,1,0:T(1,128)S(1)} %bitcast.34), channel_id=1, replica_groups={{0,8,16,24,32,40,48,56},{64,72,80,88,96,104,112,120},{128,136,144,152,1..., dimensions={0}, use_global_device_ids=true | all-gather | bytes 4608 | tf_op jit(solution)/shard_map/all_gather | solution.py:36
  88.0 15.0 %all-gather.11.cloned.1.call-done = bf16[8,8,224,128]{3,2,1,0:T(8,128)(2,1)} async-done(((bf16[2,8,224,128]{3,2,1,0:T(8,128)(2,1)}), bf16[8,8,224,128]{3,2,1,0:T(8,128)(2,1)}) %all-gather.11.cloned.1.call-update) | async-done | bytes 3670032 | tf_op jit(solution)/shard_map/all_gather | solution.py:20
  103.1 5.3 %copy.20 = bf16[4,2,8,224,128]{4,2,0,3,1:T(8,128)(2,1)} copy(bf16[4,2,8,224,128]{4,3,2,1,0:T(8,128)(2,1)} %bitcast.29) | data formatting | bytes 7340032 | tf_op jit(solution)/shard_map/all_gather | solution.py:20
  108.3 6.7 %reshape.16 = bf16[448,4096]{1,0:T(8,128)(2,1)} reshape(bf16[2,224,4,8,128]{4,3,2,1,0:T(8,128)(2,1)} %bitcast.28) | data formatting | bytes 7340032 | tf_op jit(solution)/shard_map/reshape | solution.py:21
  115.0 42.4 %all-gather.15.cloned.1.call-done = bf16[8,128,4096]{2,1,0:T(8,128)(2,1)} async-done(((bf16[8,16,4096]{2,1,0:T(8,128)(2,1)}), bf16[8,128,4096]{2,1,0:T(8,128)(2,1)}) %all-gather.15.cloned.1.call-update) | async-done | bytes 8388624 | tf_op jit(solution)/shard_map/all_gather | solution.py:26
  157.4 9.8 %fusion.10 = f32[448,1024]{1,0:T(8,128)} fusion(bf16[448,4096]{1,0:T(8,128)(2,1)} %reshape.16, bf16[1024,4096]{1,0:T(8,128)(2,1)} %bitcast.35), kind=kOutput, calls=%fused_computation.19 | convolution fusion | flops 3758096384 | bytes 13893632 | tf_op jit(solution)/shard_map/dot_general | solution.py:28
  167.2 39.8 %all-gather.9.cloned.1.call-done = f32[512,1024]{1,0:T(8,128)} async-done(((f32[512,128]{1,0:T(8,128)}), f32[512,1024]{1,0:T(8,128)}) %all-gather.9.cloned.1.call-update) | async-done | bytes 2097168 | tf_op jit(solution)/shard_map/all_gather | solution.py:35
  207.1 2.8 bitcast_reduce_fusion
  209.9 0.5 fusion
  210.4 0.2 fusion.6
  210.6 23.6 %all-reduce = f32[16,256]{1,0:T(8,128)S(1)} all-reduce(f32[16,256]{1,0:T(8,128)S(1)} %fusion.6), channel_id=5, replica_groups=mesh['dp'=32,'hidden'=8] {'hidden'}, use_global_device_ids=true, to_apply=%region_1.2.clone | all-reduce | flops 4096 | bytes 32768
  234.2 74.1 %all-reduce.1 = f32[2,256]{1,0:T(2,128)S(1)} all-reduce(f32[2,256]{1,0:T(2,128)S(1)} %constant_dynamic-slice_fusion.1), channel_id=6, replica_groups=mesh['dp'=32,'hidden'=8] {'dp'}, use_global_device_ids=true, to_apply=%region_2.3.clone | all-reduce | flops 512 | bytes 4096
  308.3 0.6 constant_dynamic-slice_fusion
  (16 shorter events, 0.0 us)
Async XLA Ops:
  6.5 200.6 %copy-start = (bf16[512,1792]{1,0:T(8,128)(2,1)S(1)}, bf16[512,1792]{1,0:T(8,128)(2,1)}, u32[]{:S(2)}) copy-start(bf16[512,1792]{1,0:T(8,128)(2,1)} %param.12) | copy-start | bytes 5505028
  6.5 49.8 %all-gather.13.cloned.1.call-start = ((), (), s32[]{:S(2)}) async-start(), calls=%async_computation.3 | async-start | bytes 1179648 | tf_op jit(solution)/shard_map/all_gather | solution.py:25
  8.3 94.8 %all-gather.11.cloned.1.call-start = ((), (), s32[]{:S(2)}) async-start(), calls=%async_computation.2 | async-start | bytes 4587520 | tf_op jit(solution)/shard_map/all_gather | solution.py:20
  50.0 6.4 %copy-start.1 = (bf16[128,4096]{1,0:T(8,128)(2,1)S(1)}, bf16[128,4096]{1,0:T(8,128)(2,1)}, u32[]{:S(2)}) copy-start(bf16[128,4096]{1,0:T(8,128)(2,1)} %param.11) | copy-start | bytes 3145732
  50.0 6.4 %copy-start.2 = (bf16[64,4096]{1,0:T(8,128)(2,1)S(1)}, bf16[64,4096]{1,0:T(8,128)(2,1)}, u32[]{:S(2)}) copy-start(bf16[64,4096]{1,0:T(8,128)(2,1)} %param.13) | copy-start | bytes 1572868
  51.0 20.7 %copy-start.6 = (u32[256]{0:T(256)S(1)}, u32[256]{0:T(256)}, u32[]{:S(2)}) copy-start(u32[256]{0:T(256)} %constant.30) | copy-start | bytes 3076
  51.0 21.3 %copy-start.5 = (u32[256]{0:T(256)S(1)}, u32[256]{0:T(256)}, u32[]{:S(2)}) copy-start(u32[256]{0:T(256)} %constant.34) | copy-start | bytes 3076
  51.0 23.2 %copy-start.3 = (s32[128]{0:T(128)S(1)}, s32[128]{0:T(128)}, u32[]{:S(2)}) copy-start(s32[128]{0:T(128)} %param.14) | copy-start | bytes 1540
  51.1 106.4 %all-gather.15.cloned.1.call-start = ((), (), s32[]{:S(2)}) async-start(), calls=%async_computation.4 | async-start | bytes 9437184 | tf_op jit(solution)/shard_map/all_gather | solution.py:26
  56.4 150.7 %all-gather.9.cloned.1.call-start = ((), (), s32[]{:S(2)}) async-start(), calls=%async_computation.1 | async-start | bytes 2359296 | tf_op jit(solution)/shard_map/all_gather | solution.py:35
  167.2 43.2 %copy-start.4 = (s32[256]{0:T(256)S(1)}, s32[256]{0:T(256)}, u32[]{:S(2)}) copy-start(s32[256]{0:T(256)} %param.15) | copy-start | bytes 3076
Sparse Core Ops, SparseCore 0:
  9.1 47.1 all-gather.12
  58.1 44.8 all-gather.10
  104.9 52.4 all-gather.14
  159.0 48.0 all-gather.8

commit v2 on v0

v2 whole, which is shorter than its diff:
```python
import jax
import jax.numpy as jnp
from jax import lax
from jax.experimental import pallas as pl
from jax.experimental.pallas import tpu as pltpu
from jax.sharding import PartitionSpec as P

MESH = pl.DeviceIdType.MESH
NT = (((1,), (1,)), ((), ()))
NX, NY, NZ = 4, 4, 8
R = 32
F = 224
DIST = (0, -1, 1, -2, 2, -3, 3, 4)
PLACE = {d: i for i, d in enumerate(DIST)}
PLACE[-4] = PLACE[4]


def kernel(
    tokens, gate, up, cot, ql, qr, ids, slot, out,
    tok, wb, rb, idb, gate_v, up_v, gate_t, up_t, cot_v, qr_v, ql_v, ids_v, slot_v,
    acc, act, scores, spread, part, got, tile, tiles,
    local_sem, z_send, x_send, c_send, w_send, y_send, r_send, tail_send,
    z_recv, x_recv, xh_recv, c_recv, w_recv, y_recv, yh_recv, rz_recv, rx_recv, rc_recv, tail_recv,
):
    dp, hid = lax.axis_index("dp"), lax.axis_index("hidden")
    y, z = dp // NZ, lax.rem(dp, NZ)
    x, c = hid // 2, lax.rem(hid, 2)
    hidden_count = 2 * NX

    def at(dx=0, dy=0, dz=0, dc=0):
        return (
            lax.rem(y + dy + NY, NY) * NZ + lax.rem(z + dz + NZ, NZ),
            lax.rem(x + dx + NX, NX) * 2 + lax.rem(c + dc, 2),
        )

    def send(src, dst, send_sem, recv_sem, **where):
        pltpu.make_async_remote_copy(
            src, dst, send_sem, recv_sem, device_id=at(**where), device_id_type=MESH
        ).start()

    def wait(ref, sem):
        pltpu.make_async_copy(ref, ref, sem).wait()

    loads = [
        pltpu.make_async_copy(gate, gate_v, local_sem.at[0]),
        pltpu.make_async_copy(up, up_v, local_sem.at[1]),
        pltpu.make_async_copy(cot, cot_v, local_sem.at[2]),
        pltpu.make_async_copy(qr, qr_v, local_sem.at[3]),
        pltpu.make_async_copy(ids, ids_v, local_sem.at[4]),
        pltpu.make_async_copy(slot, slot_v, local_sem.at[5]),
        pltpu.make_async_copy(
            ql.at[:, pl.ds(pl.multiple_of((5 * z) // 3 * 128, 128), 384)], ql_v, local_sem.at[6]
        ),
        pltpu.make_async_copy(tokens, tok.at[pl.ds(0, 128)], local_sem.at[7]),
    ]
    for load in loads:
        load.start()

    barrier = pltpu.get_barrier_semaphore()
    peers = [dict(dz=d) for d in range(1, NZ)] + [dict(dx=d) for d in range(1, NX)]
    peers += [dict(dy=1), dict(dy=-1), dict(dc=1)]
    for peer in peers:
        pl.semaphore_signal(barrier, inc=1, device_id=at(**peer), device_id_type=MESH)
    pl.semaphore_wait(barrier, len(peers))

    def rows(d, dx=0):
        first = c * 64 + lax.rem(x + dx + NX, NX) * 16
        return pl.ds(pl.multiple_of(PLACE[d] * 128 + first, 16), 16)

    half = (pl.ds(0, 2048), pl.ds(2048, 2048))
    own_rows = pl.ds(pl.multiple_of(c * 64 + x * 16, 16), 16)
    for s in (1, -1):
        send(tokens.at[own_rows], tok.at[rows(-s)], z_send, z_recv.at[PLACE[-s]], dz=s)

    loads[0].wait()
    loads[1].wait()

    @pl.loop(0, 14)
    def _(i):
        at_tile = pl.ds(pl.multiple_of(i * 128, 128), 128)
        gate_t[at_tile, :] = gate_v[:, at_tile].T
        up_t[at_tile, :] = up_v[:, at_tile].T

    def window(dz=0, dy=0):
        return lax.rem(y + dy + NY, NY) * NZ + lax.rem(z + dz + NZ, NZ)

    def units(dz):
        return pl.ds(pl.multiple_of(lax.rem(z + dz + NZ, NZ) * F, 32), F)

    upper, lower = pl.ds(0, F), pl.ds(F, F)
    for s in (1, -1):
        send(gate_t.at[units(0)], wb.at[dp, upper], y_send, y_recv.at[0, (1 - s) // 2], dy=s)
        send(up_t.at[units(0)], wb.at[dp, lower], y_send, y_recv.at[0, (1 - s) // 2], dy=s)
    for d in (1, -1, 2, -2, 3, -3, 4):
        send(gate_t.at[units(d)], wb.at[dp, upper], w_send, w_recv.at[PLACE[-d]], dz=d)
        send(up_t.at[units(d)], wb.at[dp, lower], w_send, w_recv.at[PLACE[-d]], dz=d)
    wb[dp, upper, :] = gate_t[units(0), :]
    wb[dp, lower, :] = up_t[units(0), :]

    loads[2].wait()
    loads[3].wait()
    query_rows = pl.ds(pl.multiple_of(hid * 64, 64), 64)

    def k_rows(dx=0, dc=0):
        first = lax.rem(c + dc, 2) * 256 + lax.rem(x + dx + NX, NX) * 64
        return pl.ds(pl.multiple_of(first, 64), 64)

    rb[0, k_rows(), :] = lax.dot_general(
        qr_v[...], cot_v[...], NT, preferred_element_type=jnp.float32
    )
    loads[4].wait()
    idb[0] = ids_v[...]
    for d in (1, -1, 2, -2, 3, -3, 4):
        send(rb.at[0, k_rows()], rb.at[PLACE[-d], k_rows()], r_send.at[0], rz_recv.at[PLACE[-d]], dz=d)
        send(ids_v, idb.at[PLACE[-d]], r_send.at[1], rz_recv.at[PLACE[-d] + NZ], dz=d)

    def right_along_x(place):
        for d in (1, -1, 2):
            send(rb.at[place, k_rows()], rb.at[place, k_rows()], r_send.at[2], rx_recv.at[place], dx=d)

    def tokens_along_x(d):
        for s in (1, -1):
            send(tok.at[rows(d)], tok.at[rows(d)], x_send, x_recv.at[PLACE[d], (1 - s) // 2], dx=s)

    def pass_tokens(d):
        for s in (1, -1):
            i = (1 - s) // 2
            wait(tok.at[rows(d)], x_recv.at[PLACE[d], i])
            piece = tok.at[rows(d, -s), half[i]]
            send(piece, piece, x_send, xh_recv.at[PLACE[d], i], dx=s)

    def swap_cores(d):
        place = PLACE[d]
        for i in range(2):
            wait(tok.at[rows(d), half[i]], xh_recv.at[place, i])
        mine = tok.at[pl.ds(pl.multiple_of(place * 128 + c * 64, 16), 64)]
        send(mine, mine, c_send.at[0], c_recv.at[place], dc=1)
        wait(rb.at[place, pl.ds(0, 192)], rx_recv.at[place])
        mine = rb.at[place, pl.ds(pl.multiple_of(c * 256, 256), 256)]
        send(mine, mine, c_send.at[1], rc_recv.at[place], dc=1)

    def weights_along_y(d):
        piece = wb.at[window(d)]
        for s in (1, -1):
            send(piece, piece, y_send, y_recv.at[PLACE[d], (1 - s) // 2], dy=s)

    def pass_weights(d):
        for s in (1, -1):
            i = (1 - s) // 2
            wait(wb.at[dp], y_recv.at[PLACE[d], i])
            piece = wb.at[window(d, -s), (upper, lower)[i]]
            send(piece, piece, y_send, yh_recv.at[PLACE[d], i], dy=s)

    right_along_x(0)
    for g in range(1, 7):
        for d in (-g, g):
            if g < 4:
                s = 1 if d < 0 else -1
                place = PLACE[d]
                wait(tok.at[rows(d)], z_recv.at[place])
                if g < 3:
                    send(tok.at[rows(d)], tok.at[rows(d - s)], z_send, z_recv.at[PLACE[d - s]], dz=s)
                else:
                    i = (1 - s) // 2
                    send(
                        tok.at[rows(d), half[i]], tok.at[rows(4), half[i]], z_send,
                        z_recv.at[NZ - 1 + i], dz=s,
                    )
                tokens_along_x(d)
        if g == 4:
            for i in range(2):
                wait(tok.at[rows(4), half[i]], z_recv.at[NZ - 1 + i])
            tokens_along_x(4)
        for d in (-g, g) if g < 4 else (4,) if g == 4 else ():
            wait(wb.at[dp], w_recv.at[PLACE[d]])
            weights_along_y(d)
        for d in (-g, g) if g < 4 else (4,) if g == 4 else ():
            wait(rb.at[0, pl.ds(0, 64)], rz_recv.at[PLACE[d]])
            wait(idb.at[0], rz_recv.at[PLACE[d] + NZ])
            right_along_x(PLACE[d])
        h = g - 1
        for d in (0,) if h == 0 else (-h, h) if h < 4 else (4,) if h == 4 else ():
            pass_weights(d)
            if h > 0:
                pass_tokens(d)
        h = g - 2
        for d in (-h, h) if 0 < h < 4 else (4,) if h == 4 else ():
            swap_cores(d)

    loads[5].wait()
    columns = lax.broadcasted_iota(jnp.int32, (256, 256), 0)
    placing = (columns == slot_v[...]).astype(jnp.float32).astype(jnp.bfloat16)
    docs = lax.broadcasted_iota(jnp.int32, (256, 128), 0)
    for place in range(NZ):
        one_hot = (docs == idb[place]).astype(jnp.float32).astype(jnp.bfloat16)
        spread[:, pl.ds(place * 128, 128)] = jnp.dot(
            placing, one_hot, preferred_element_type=jnp.float32
        ).astype(jnp.bfloat16)

    wait(rb.at[0, pl.ds(0, 192)], rx_recv.at[0])
    mine = rb.at[0, pl.ds(pl.multiple_of(c * 256, 256), 256)]
    send(mine, mine, c_send.at[1], rc_recv.at[0], dc=1)
    for d in DIST:
        for i in range(2):
            wait(wb.at[dp, upper], yh_recv.at[PLACE[d], i])
        if d != 0:
            wait(tok.at[pl.ds(0, 64)], c_recv.at[PLACE[d]])
        wait(rb.at[0, pl.ds(0, 256)], rc_recv.at[PLACE[d]])
    loads[6].wait()
    loads[7].wait()
    act[...] = jnp.zeros_like(act)
    scores[...] = jnp.zeros_like(scores)
    first = pl.multiple_of(F * z - (5 * z) // 3 * 128, 32)

    @pl.loop(0, 4)
    def _(j):
        span = pl.ds(pl.multiple_of(j * 256, 256), 256)
        acc[...] = jnp.zeros_like(acc)

        @pl.loop(0, 4)
        def _(k):
            weights = jnp.concatenate([wb[k * 8 + i] for i in range(8)], axis=1)
            inputs = tok[span, pl.ds(pl.multiple_of(k * 1024, 1024), 1024)]
            acc[...] += lax.dot_general(weights, inputs, NT, preferred_element_type=jnp.float32)

        gates = acc[:F]
        act[pl.ds(first, F), :] = (gates / (1.0 + jnp.exp(-gates)) * acc[F:]).astype(jnp.bfloat16)
        left = jnp.dot(ql_v[...], act[...], preferred_element_type=jnp.float32)
        for q in range(16):
            where = (q % 4 // 2 * 64 + q % 2 * 32) + (q // 4) * 128
            hidden = where // 64
            at_row = hidden % 2 * 256 + hidden // 2 * 64 + where % 64
            right = jnp.concatenate(
                [rb[2 * j, at_row:at_row + R], rb[2 * j + 1, at_row:at_row + R]], axis=1
            )
            scores[q:q + 1, span] = jnp.sum(
                left[q * R:(q + 1) * R] * right, axis=0, keepdims=True
            )

    rest = scores[...]
    columns_sum = jnp.zeros((256, 128), jnp.float32)
    for _ in range(3):
        rounded = rest.astype(jnp.bfloat16)
        rest = rest - rounded.astype(jnp.float32)
        columns_sum += lax.dot_general(spread[...], rounded, NT, preferred_element_type=jnp.float32)
    part[...] = columns_sum.reshape(32, 8, 128)

    @pl.loop(1, 32)
    def _(k):
        to = lax.rem(dp + k, 32)
        pltpu.make_async_remote_copy(
            part.at[to], got.at[dp], tail_send.at[0], tail_recv.at[0],
            device_id=(to, hid), device_id_type=MESH,
        ).start()

    wait(got.at[pl.ds(0, 31)], tail_recv.at[0])
    got[dp] = part[dp]
    tile[...] = jnp.sum(got[...], axis=0)
    for k in range(1, hidden_count):
        pltpu.make_async_remote_copy(
            tile, tiles.at[hid], tail_send.at[1], tail_recv.at[1],
            device_id=(dp, lax.rem(hid + k, hidden_count)), device_id_type=MESH,
        ).start()
    wait(tiles.at[pl.ds(0, hidden_count - 1)], tail_recv.at[1])
    tiles[hid] = tile[...]
    total = jnp.sum(tiles[...], axis=0)
    query = lax.broadcasted_iota(jnp.int32, (8, 128), 0) + 2 * hid
    pick = (lax.broadcasted_iota(jnp.int32, (8, 128), 1) == query).astype(jnp.float32)
    result = lax.dot_general(
        pick, total, NT, precision=lax.Precision.HIGHEST, preferred_element_type=jnp.float32
    )
    out[...] = result[:2]

    wait(tok.at[pl.ds(0, 7 * 16)], z_send)
    wait(tok.at[pl.ds(0, 7 * 48)], x_send)
    wait(tok.at[pl.ds(0, 7 * 64)], c_send.at[0])
    wait(rb.at[:, pl.ds(0, 256)], c_send.at[1])
    wait(wb.at[pl.ds(0, 7)], w_send)
    wait(wb.at[pl.ds(0, 24)], y_send)
    wait(rb.at[pl.ds(0, 7), pl.ds(0, 64)], r_send.at[0])
    wait(idb.at[pl.ds(0, 7)], r_send.at[1])
    wait(rb.at[:, pl.ds(0, 192)], r_send.at[2])
    wait(got.at[pl.ds(0, 31)], tail_send.at[0])
    wait(tiles.at[pl.ds(0, hidden_count - 1)], tail_send.at[1])


def local(tokens, gate_weight, up_weight, cotangent, query_left, query_right, doc_ids, doc_slot):
    bf16, f32, i32 = jnp.bfloat16, jnp.float32, jnp.int32
    dma = pltpu.SemaphoreType.DMA
    anywhere = pl.BlockSpec(memory_space=pl.ANY)
    return pl.pallas_call(
        kernel,
        out_shape=jax.ShapeDtypeStruct((2, 8), f32),
        in_specs=[anywhere] * 8,
        out_specs=pl.BlockSpec(memory_space=pltpu.VMEM),
        scratch_shapes=[
            pltpu.VMEM((1024, 4096), bf16),
            pltpu.VMEM((32, 2 * F, 128), bf16),
            pltpu.VMEM((8, 512, 128), f32),
            pltpu.VMEM((8, 1, 128), i32),
            pltpu.VMEM((128, 1792), bf16),
            pltpu.VMEM((128, 1792), bf16),
            pltpu.VMEM((1792, 128), bf16),
            pltpu.VMEM((1792, 128), bf16),
            pltpu.VMEM((128, 4096), bf16),
            pltpu.VMEM((64, 4096), bf16),
            pltpu.VMEM((512, 384), bf16),
            pltpu.VMEM((1, 128), i32),
            pltpu.VMEM((1, 256), i32),
            pltpu.VMEM((2 * F, 256), f32),
            pltpu.VMEM((384, 256), bf16),
            pltpu.VMEM((128, 1024), f32),
            pltpu.VMEM((256, 1024), bf16),
            pltpu.VMEM((32, 8, 128), f32),
            pltpu.VMEM((32, 8, 128), f32),
            pltpu.VMEM((8, 128), f32),
            pltpu.VMEM((8, 8, 128), f32),
            dma((8,)), dma, dma, dma((2,)), dma, dma, dma((3,)), dma((2,)),
            dma((9,)), dma((8, 2)), dma((8, 2)), dma((8,)), dma((8,)), dma((8, 2)), dma((8, 2)),
            dma((16,)), dma((8,)), dma((8,)), dma((2,)),
        ],
        compiler_params=pltpu.CompilerParams(
            collective_id=0, has_side_effects=True, vmem_limit_bytes=48 * 1024 * 1024
        ),
        name="influence",
    )(
        tokens, gate_weight, up_weight, cotangent, query_left, query_right,
        doc_ids.reshape(1, -1), doc_slot.reshape(1, -1),
    )


def solution(mesh):
    return jax.shard_map(
        local,
        mesh=mesh,
        in_specs=(
            P("dp", None),
            P("dp", "hidden"),
            P("dp", "hidden"),
            P("dp", None),
            P(None, "hidden"),
            P("hidden", None),
            P("dp"),
            P(),
        ),
        out_specs=P("hidden", "dp"),
        check_vma=False,
    )
```

time: 427 us -> 108 us (0.25)
  the two profiles are of different devices: /device:TPU:0 before, /device:TPU:1 now
where the time goes in v2:
time: 108 us
  Pallas kernels  98.9 us (92%)
  local copies, waits for them, and re-layouts  8.92 us (8%)
    pallas_call x1, Pallas kernels, local(): pl.pallas_call(kernel, out_shape=jax.ShapeDtypeStruct((2, 8), f32), in_sp...  98.9 us
    unnamed x17, local copies, waits for them, and re-layouts  8.92 us

profile of v2, /device:TPU:1, one launch (start us, length us, event | category | flops | bytes accessed | tf_op | source)
XLA Modules:
  0.0 107.9 jit_solution(9728081675594158154)
XLA Ops:
  0.0 0.0 copy-start
  0.0 1.5 %copy-done = bf16[512,1792]{1,0:T(8,128)(2,1)S(1)} copy-done((bf16[512,1792]{1,0:T(8,128)(2,1)S(1)}, bf16[512,1792]{1,0:T(8,128)(2,1)}, u32[]{:S(2)}) %copy-start) | copy-done | bytes 1835032
  1.5 0.0 copy-start.1
  1.5 1.2 %copy-done.1 = bf16[128,4096]{1,0:T(8,128)(2,1)S(1)} copy-done((bf16[128,4096]{1,0:T(8,128)(2,1)S(1)}, bf16[128,4096]{1,0:T(8,128)(2,1)}, u32[]{:S(2)}) %copy-start.1) | copy-done | bytes 1048600
  2.7 0.0 copy-start.2
  2.7 1.2 %copy-done.2 = bf16[128,4096]{1,0:T(8,128)(2,1)S(1)} copy-done((bf16[128,4096]{1,0:T(8,128)(2,1)S(1)}, bf16[128,4096]{1,0:T(8,128)(2,1)}, u32[]{:S(2)}) %copy-start.2) | copy-done | bytes 1048600
  4.0 0.0 copy-start.3
  4.0 1.0 copy-done.3
  5.0 0.0 copy-start.4
  5.0 1.0 copy-done.4
  6.0 0.0 copy-start.5
  6.0 1.0 copy-done.5
  7.0 0.0 copy-start.6
  7.0 0.7 copy-done.6
  7.7 0.0 copy-start.7
  7.7 0.7 copy-done.7
  8.4 98.9 %influence.1 = f32[2,8]{1,0:T(2,128)S(1)} custom-call(bf16[128,4096]{1,0:T(8,128)(2,1)S(1)} %copy-done.1, bf16[128,1792]{1,0:T(8,128)(2,1)S(1)} %copy-done.4, bf16[128,1792]{1,0:T(8,128)(2,1)S(1)} %copy-done.5, bf16[128,4096]{1,0:T(8,128)(2,1)S(1)} %copy-done.2, bf16[512,1792]{1,0:T(8,128)(2,1)S(1)} %copy-done, bf16[64,4096]{1,0:T(8,128)(2,1)S(1)} %copy-done.3, ...), custom_call_target="tpu_custom_call" | custom-call | tf_op jit(solution)/shard_map/influence/pallas_call | solution.py:291
  107.3 0.6 copy.10
Async XLA Ops:
  0.0 1.5 %copy-start = (bf16[512,1792]{1,0:T(8,128)(2,1)S(1)}, bf16[512,1792]{1,0:T(8,128)(2,1)}, u32[]{:S(2)}) copy-start(bf16[512,1792]{1,0:T(8,128)(2,1)} %ql.1) | copy-start | bytes 5505028
  1.5 1.2 %copy-start.1 = (bf16[128,4096]{1,0:T(8,128)(2,1)S(1)}, bf16[128,4096]{1,0:T(8,128)(2,1)}, u32[]{:S(2)}) copy-start(bf16[128,4096]{1,0:T(8,128)(2,1)} %tokens.1) | copy-start | bytes 3145732
  2.7 1.2 %copy-start.2 = (bf16[128,4096]{1,0:T(8,128)(2,1)S(1)}, bf16[128,4096]{1,0:T(8,128)(2,1)}, u32[]{:S(2)}) copy-start(bf16[128,4096]{1,0:T(8,128)(2,1)} %cot.1) | copy-start | bytes 3145732
  4.0 1.0 copy-start.3
  5.0 1.0 copy-start.4
  6.0 1.0 copy-start.5
  7.0 0.7 copy-start.6
  7.7 0.7 copy-start.7

commit v3 on v2

--- a/solution.py
+++ b/solution.py
@@ -17,10 +17,11 @@
 
 def kernel(
     tokens, gate, up, cot, ql, qr, ids, slot, out,
-    tok, wb, rb, idb, gate_v, up_v, gate_t, up_t, cot_v, qr_v, ql_v, ids_v, slot_v,
+    tok, wb, rb, sb, idb, gate_v, up_v, gate_t, up_t, cot_v, qr_v, ql_v, ids_v, slot_v,
     acc, act, scores, spread, part, got, tile, tiles,
     local_sem, z_send, x_send, c_send, w_send, y_send, r_send, tail_send,
-    z_recv, x_recv, xh_recv, c_recv, w_recv, y_recv, yh_recv, rz_recv, rx_recv, rc_recv, tail_recv,
+    z_recv, x_recv, xh_recv, c_recv, w_recv, y_recv, yh_recv,
+    rz_recv, rx_recv, rxh_recv, rc_recv, tail_recv,
 ):
     dp, hid = lax.axis_index("dp"), lax.axis_index("hidden")
     y, z = dp // NZ, lax.rem(dp, NZ)
@@ -57,8 +58,7 @@
         load.start()
 
     barrier = pltpu.get_barrier_semaphore()
-    peers = [dict(dz=d) for d in range(1, NZ)] + [dict(dx=d) for d in range(1, NX)]
-    peers += [dict(dy=1), dict(dy=-1), dict(dc=1)]
+    peers = [dict(dz=1), dict(dz=-1), dict(dx=1), dict(dx=-1), dict(dy=1), dict(dy=-1), dict(dc=1)]
     for peer in peers:
         pl.semaphore_signal(barrier, inc=1, device_id=at(**peer), device_id_type=MESH)
     pl.semaphore_wait(barrier, len(peers))
@@ -88,35 +88,77 @@
         return pl.ds(pl.multiple_of(lax.rem(z + dz + NZ, NZ) * F, 32), F)
 
     upper, lower = pl.ds(0, F), pl.ds(F, F)
+
+    def exchange_weights(d):
+        send(gate_t.at[units(d)], wb.at[dp, upper], w_send, w_recv.at[PLACE[-d]], dz=d)
+        send(up_t.at[units(d)], wb.at[dp, lower], w_send, w_recv.at[PLACE[-d]], dz=d)
+
     for s in (1, -1):
         send(gate_t.at[units(0)], wb.at[dp, upper], y_send, y_recv.at[0, (1 - s) // 2], dy=s)
         send(up_t.at[units(0)], wb.at[dp, lower], y_send, y_recv.at[0, (1 - s) // 2], dy=s)
-    for d in (1, -1, 2, -2, 3, -3, 4):
-        send(gate_t.at[units(d)], wb.at[dp, upper], w_send, w_recv.at[PLACE[-d]], dz=d)
-        send(up_t.at[units(d)], wb.at[dp, lower], w_send, w_recv.at[PLACE[-d]], dz=d)
+    for d in (1, -1):
+        exchange_weights(d)
     wb[dp, upper, :] = gate_t[units(0), :]
     wb[dp, lower, :] = up_t[units(0), :]
 
     loads[2].wait()
     loads[3].wait()
-    query_rows = pl.ds(pl.multiple_of(hid * 64, 64), 64)
-
-    def k_rows(dx=0, dc=0):
-        first = lax.rem(c + dc, 2) * 256 + lax.rem(x + dx + NX, NX) * 64
-        return pl.ds(pl.multiple_of(first, 64), 64)
-
-    rb[0, k_rows(), :] = lax.dot_general(
-        qr_v[...], cot_v[...], NT, preferred_element_type=jnp.float32
-    )
+
+    def k_rows(dx=0, first=0, count=64):
+        start = c * 256 + lax.rem(x + dx + NX, NX) * 64 + first
+        return pl.ds(pl.multiple_of(start, count), count)
+
+    def scale_row(dx=0):
+        return pl.ds(c * 4 + lax.rem(x + dx + NX, NX), 1)
+
+    right = lax.dot_general(qr_v[...], cot_v[...], NT, preferred_element_type=jnp.float32)
+    largest = jnp.maximum(jnp.max(jnp.abs(right), axis=0, keepdims=True), 1e-30)
+    steps = right * (32000.0 / largest)
+    steps = steps + jnp.where(steps >= 0, 0.5, -0.5)
+    rb[0, k_rows(), :] = steps.astype(jnp.int32).astype(jnp.int16)
+    sb[0, c * 4 + x] = largest / 32000.0
     loads[4].wait()
     idb[0] = ids_v[...]
-    for d in (1, -1, 2, -2, 3, -3, 4):
-        send(rb.at[0, k_rows()], rb.at[PLACE[-d], k_rows()], r_send.at[0], rz_recv.at[PLACE[-d]], dz=d)
-        send(ids_v, idb.at[PLACE[-d]], r_send.at[1], rz_recv.at[PLACE[-d] + NZ], dz=d)
-
-    def right_along_x(place):
-        for d in (1, -1, 2):
-            send(rb.at[place, k_rows()], rb.at[place, k_rows()], r_send.at[2], rx_recv.at[place], dx=d)
+
+    def right_along_z(d, s):
+        to = PLACE[d - s]
+        here = PLACE[d]
+        send(rb.at[here, k_rows()], rb.at[to, k_rows()], r_send.at[0], rz_recv.at[0, to], dz=s)
+        send(sb.at[here, scale_row()], sb.at[to, scale_row()], r_send.at[1], rz_recv.at[1, to], dz=s)
+        send(idb.at[here], idb.at[to], r_send.at[2], rz_recv.at[2, to], dz=s)
+
+    def group(g):
+        return (0,) if g == 0 else (4,) if g == 4 else (-g, g)
+
+    def places(g):
+        return pl.ds(PLACE[group(g)[0]], len(group(g)))
+
+    def right_along_x(g):
+        for s in (1, -1):
+            i = (1 - s) // 2
+            mine = rb.at[places(g), k_rows()]
+            send(mine, mine, r_send.at[3], rx_recv.at[0, g, i], dx=s)
+            mine = sb.at[places(g), scale_row()]
+            send(mine, mine, r_send.at[4], rx_recv.at[1, g, i], dx=s)
+
+    def pass_right(g):
+        for s in (1, -1):
+            i = (1 - s) // 2
+            wait(rb.at[places(g), k_rows(-s)], rx_recv.at[0, g, i])
+            wait(sb.at[places(g), scale_row(-s)], rx_recv.at[1, g, i])
+            piece = rb.at[places(g), k_rows(-s, 32 * i, 32)]
+            send(piece, piece, r_send.at[5], rxh_recv.at[i, g], dx=s)
+        piece = sb.at[places(g), scale_row(-1)]
+        send(piece, piece, r_send.at[6], rxh_recv.at[2, g], dx=1)
+
+    def swap_right(g):
+        for i in range(2):
+            wait(rb.at[places(g), k_rows(2, 32 * i, 32)], rxh_recv.at[i, g])
+        wait(sb.at[places(g), scale_row(2)], rxh_recv.at[2, g])
+        mine = rb.at[places(g), pl.ds(pl.multiple_of(c * 256, 256), 256)]
+        send(mine, mine, c_send.at[1], rc_recv.at[0, g], dc=1)
+        mine = sb.at[places(g), pl.ds(c * 4, 4)]
+        send(mine, mine, c_send.at[2], rc_recv.at[1, g], dc=1)
 
     def tokens_along_x(d):
         for s in (1, -1):
@@ -135,9 +177,6 @@
             wait(tok.at[rows(d), half[i]], xh_recv.at[place, i])
         mine = tok.at[pl.ds(pl.multiple_of(place * 128 + c * 64, 16), 64)]
         send(mine, mine, c_send.at[0], c_recv.at[place], dc=1)
-        wait(rb.at[place, pl.ds(0, 192)], rx_recv.at[place])
-        mine = rb.at[place, pl.ds(pl.multiple_of(c * 256, 256), 256)]
-        send(mine, mine, c_send.at[1], rc_recv.at[place], dc=1)
 
     def weights_along_y(d):
         piece = wb.at[window(d)]
@@ -151,10 +190,12 @@
             piece = wb.at[window(d, -s), (upper, lower)[i]]
             send(piece, piece, y_send, yh_recv.at[PLACE[d], i], dy=s)
 
+    for s in (1, -1):
+        right_along_z(0, s)
     right_along_x(0)
     for g in range(1, 7):
-        for d in (-g, g):
-            if g < 4:
+        if g < 4:
+            for d in group(g):
                 s = 1 if d < 0 else -1
                 place = PLACE[d]
                 wait(tok.at[rows(d)], z_recv.at[place])
@@ -167,25 +208,36 @@
                         z_recv.at[NZ - 1 + i], dz=s,
                     )
                 tokens_along_x(d)
+            for d in group(g + 1):
+                exchange_weights(d)
         if g == 4:
             for i in range(2):
                 wait(tok.at[rows(4), half[i]], z_recv.at[NZ - 1 + i])
             tokens_along_x(4)
-        for d in (-g, g) if g < 4 else (4,) if g == 4 else ():
-            wait(wb.at[dp], w_recv.at[PLACE[d]])
-            weights_along_y(d)
-        for d in (-g, g) if g < 4 else (4,) if g == 4 else ():
-            wait(rb.at[0, pl.ds(0, 64)], rz_recv.at[PLACE[d]])
-            wait(idb.at[0], rz_recv.at[PLACE[d] + NZ])
-            right_along_x(PLACE[d])
+        if g <= 4:
+            for d in group(g):
+                for i in range(3):
+                    wait((rb.at[0, k_rows()], sb.at[0, scale_row()], idb.at[0])[i], rz_recv.at[i, PLACE[d]])
+                s = 1 if d < 0 else -1
+                if g < 3 or d == -3:
+                    right_along_z(d, s)
+            right_along_x(g)
+            for d in group(g):
+                wait(wb.at[dp], w_recv.at[PLACE[d]])
+                weights_along_y(d)
         h = g - 1
-        for d in (0,) if h == 0 else (-h, h) if h < 4 else (4,) if h == 4 else ():
-            pass_weights(d)
+        if h <= 4:
+            for d in group(h):
+                pass_weights(d)
+                if h > 0:
+                    pass_tokens(d)
+            pass_right(h)
+        h = g - 2
+        if 0 <= h <= 4:
             if h > 0:
-                pass_tokens(d)
-        h = g - 2
-        for d in (-h, h) if 0 < h < 4 else (4,) if h == 4 else ():
-            swap_cores(d)
+                for d in group(h):
+                    swap_cores(d)
+            swap_right(h)
 
     loads[5].wait()
     columns = lax.broadcasted_iota(jnp.int32, (256, 256), 0)
@@ -197,15 +249,14 @@
             placing, one_hot, preferred_element_type=jnp.float32
         ).astype(jnp.bfloat16)
 
-    wait(rb.at[0, pl.ds(0, 192)], rx_recv.at[0])
-    mine = rb.at[0, pl.ds(pl.multiple_of(c * 256, 256), 256)]
-    send(mine, mine, c_send.at[1], rc_recv.at[0], dc=1)
     for d in DIST:
         for i in range(2):
             wait(wb.at[dp, upper], yh_recv.at[PLACE[d], i])
         if d != 0:
             wait(tok.at[pl.ds(0, 64)], c_recv.at[PLACE[d]])
-        wait(rb.at[0, pl.ds(0, 256)], rc_recv.at[PLACE[d]])
+    for g in range(5):
+        wait(rb.at[places(g), pl.ds(0, 256)], rc_recv.at[0, g])
+        wait(sb.at[places(g), pl.ds(0, 4)], rc_recv.at[1, g])
     loads[6].wait()
     loads[7].wait()
     act[...] = jnp.zeros_like(act)
@@ -227,11 +278,15 @@
         act[pl.ds(first, F), :] = (gates / (1.0 + jnp.exp(-gates)) * acc[F:]).astype(jnp.bfloat16)
         left = jnp.dot(ql_v[...], act[...], preferred_element_type=jnp.float32)
         for q in range(16):
-            where = (q % 4 // 2 * 64 + q % 2 * 32) + (q // 4) * 128
-            hidden = where // 64
-            at_row = hidden % 2 * 256 + hidden // 2 * 64 + where % 64
+            hidden = q // 2
+            at_row = hidden % 2 * 256 + hidden // 2 * 64 + q % 2 * R
             right = jnp.concatenate(
-                [rb[2 * j, at_row:at_row + R], rb[2 * j + 1, at_row:at_row + R]], axis=1
+                [
+                    rb[2 * j + i, at_row:at_row + R].astype(jnp.int32).astype(jnp.float32)
+                    * sb[2 * j + i, hidden % 2 * 4 + hidden // 2]
+                    for i in range(2)
+                ],
+                axis=1,
             )
             scores[q:q + 1, span] = jnp.sum(
                 left[q * R:(q + 1) * R] * right, axis=0, keepdims=True
@@ -275,11 +330,16 @@
     wait(tok.at[pl.ds(0, 7 * 48)], x_send)
     wait(tok.at[pl.ds(0, 7 * 64)], c_send.at[0])
     wait(rb.at[:, pl.ds(0, 256)], c_send.at[1])
+    wait(sb.at[:, pl.ds(0, 4)], c_send.at[2])
     wait(wb.at[pl.ds(0, 7)], w_send)
     wait(wb.at[pl.ds(0, 24)], y_send)
     wait(rb.at[pl.ds(0, 7), pl.ds(0, 64)], r_send.at[0])
-    wait(idb.at[pl.ds(0, 7)], r_send.at[1])
-    wait(rb.at[:, pl.ds(0, 192)], r_send.at[2])
+    wait(sb.at[pl.ds(0, 7), pl.ds(0, 1)], r_send.at[1])
+    wait(idb.at[pl.ds(0, 7)], r_send.at[2])
+    wait(rb.at[:, pl.ds(0, 128)], r_send.at[3])
+    wait(sb.at[:, pl.ds(0, 2)], r_send.at[4])
+    wait(rb.at[:, pl.ds(0, 64)], r_send.at[5])
+    wait(sb.at[:, pl.ds(0, 1)], r_send.at[6])
     wait(got.at[pl.ds(0, 31)], tail_send.at[0])
     wait(tiles.at[pl.ds(0, hidden_count - 1)], tail_send.at[1])
 
@@ -287,7 +347,7 @@
 def local(tokens, gate_weight, up_weight, cotangent, query_left, query_right, doc_ids, doc_slot):
     bf16, f32, i32 = jnp.bfloat16, jnp.float32, jnp.int32
     dma = pltpu.SemaphoreType.DMA
-    anywhere = pl.BlockSpec(memory_space=pl.ANY)
+    anywhere = pl.BlockSpec(memory_space=pltpu.HBM)
     return pl.pallas_call(
         kernel,
         out_shape=jax.ShapeDtypeStruct((2, 8), f32),
@@ -296,7 +356,8 @@
         scratch_shapes=[
             pltpu.VMEM((1024, 4096), bf16),
             pltpu.VMEM((32, 2 * F, 128), bf16),
-            pltpu.VMEM((8, 512, 128), f32),
+            pltpu.VMEM((8, 512, 128), jnp.int16),
+            pltpu.VMEM((8, 8, 1, 128), f32),
             pltpu.VMEM((8, 1, 128), i32),
             pltpu.VMEM((128, 1792), bf16),
             pltpu.VMEM((128, 1792), bf16),
@@ -315,12 +376,12 @@
             pltpu.VMEM((32, 8, 128), f32),
             pltpu.VMEM((8, 128), f32),
             pltpu.VMEM((8, 8, 128), f32),
-            dma((8,)), dma, dma, dma((2,)), dma, dma, dma((3,)), dma((2,)),
+            dma((8,)), dma, dma, dma((3,)), dma, dma, dma((7,)), dma((2,)),
             dma((9,)), dma((8, 2)), dma((8, 2)), dma((8,)), dma((8,)), dma((8, 2)), dma((8, 2)),
-            dma((16,)), dma((8,)), dma((8,)), dma((2,)),
+            dma((3, 8)), dma((2, 5, 2)), dma((3, 5)), dma((2, 5)), dma((2,)),
         ],
         compiler_params=pltpu.CompilerParams(
-            collective_id=0, has_side_effects=True, vmem_limit_bytes=48 * 1024 * 1024
+            collective_id=0, has_side_effects=True, vmem_limit_bytes=60 * 1024 * 1024
         ),
         name="influence",
     )(

time: 108 us -> 78.6 us (0.73)
  Pallas kernels: 98.9 us -> 77.3 us
  local copies, waits for them, and re-layouts: 8.92 us -> 1.24 us
    pallas_call x1, Pallas kernels: 98.9 us -> 77.3 us  [local(): pl.pallas_call(kernel, out_shape=jax.ShapeDtypeStruct((2, 8), f32), in_sp...]
    unnamed x17 -> x1, local copies, waits for them, and re-layouts: 8.92 us -> 1.24 us
where the time goes in v3:
time: 78.6 us
  Pallas kernels  77.3 us (98%)
  local copies, waits for them, and re-layouts  1.24 us (2%)
    pallas_call x1, Pallas kernels, local(): pl.pallas_call(kernel, out_shape=jax.ShapeDtypeStruct((2, 8), f32), in_sp...  77.3 us

profile of v3, /device:TPU:1, one launch (start us, length us, event | category | flops | bytes accessed | tf_op | source)
XLA Modules:
  0.0 78.6 jit_solution(10708848743290969613)
XLA Ops:
  0.0 77.3 %influence.1 = f32[2,8]{1,0:T(2,128)} custom-call(bf16[128,4096]{1,0:T(8,128)(2,1)} %tokens.1, bf16[128,1792]{1,0:T(8,128)(2,1)} %gate.1, bf16[128,1792]{1,0:T(8,128)(2,1)} %up.1, bf16[128,4096]{1,0:T(8,128)(2,1)} %cot.1, bf16[512,1792]{1,0:T(8,128)(2,1)} %ql.1, bf16[64,4096]{1,0:T(8,128)(2,1)} %qr.1, s32[1,128]{1,0:T(1,128)} %bitcast.3, s32[1,256]{1,0:T(1,128)} %bitcast.2), custom_call_target="tpu_custom_call" | custom-call | tf_op jit(solution)/shard_map/influence/pallas_call | solution.py:351
  77.3 1.2 %copy.10 = f32[2,8]{1,0:T(2,128)} copy(f32[2,8]{1,0:T(2,128)} %influence.1) | data formatting | bytes 128

commit v4 on v3

--- a/solution.py
+++ b/solution.py
@@ -69,37 +69,12 @@
 
     half = (pl.ds(0, 2048), pl.ds(2048, 2048))
     own_rows = pl.ds(pl.multiple_of(c * 64 + x * 16, 16), 16)
-    for s in (1, -1):
-        send(tokens.at[own_rows], tok.at[rows(-s)], z_send, z_recv.at[PLACE[-s]], dz=s)
-
-    loads[0].wait()
-    loads[1].wait()
-
-    @pl.loop(0, 14)
-    def _(i):
-        at_tile = pl.ds(pl.multiple_of(i * 128, 128), 128)
-        gate_t[at_tile, :] = gate_v[:, at_tile].T
-        up_t[at_tile, :] = up_v[:, at_tile].T
-
-    def window(dz=0, dy=0):
-        return lax.rem(y + dy + NY, NY) * NZ + lax.rem(z + dz + NZ, NZ)
-
-    def units(dz):
-        return pl.ds(pl.multiple_of(lax.rem(z + dz + NZ, NZ) * F, 32), F)
-
-    upper, lower = pl.ds(0, F), pl.ds(F, F)
-
-    def exchange_weights(d):
-        send(gate_t.at[units(d)], wb.at[dp, upper], w_send, w_recv.at[PLACE[-d]], dz=d)
-        send(up_t.at[units(d)], wb.at[dp, lower], w_send, w_recv.at[PLACE[-d]], dz=d)
-
-    for s in (1, -1):
-        send(gate_t.at[units(0)], wb.at[dp, upper], y_send, y_recv.at[0, (1 - s) // 2], dy=s)
-        send(up_t.at[units(0)], wb.at[dp, lower], y_send, y_recv.at[0, (1 - s) // 2], dy=s)
-    for d in (1, -1):
-        exchange_weights(d)
-    wb[dp, upper, :] = gate_t[units(0), :]
-    wb[dp, lower, :] = up_t[units(0), :]
+    for i in range(2):
+        for s in (1, -1):
+            send(
+                tokens.at[own_rows, half[i]], tok.at[rows(-s), half[i]], z_send,
+                z_recv.at[PLACE[-s], i], dz=s,
+            )
 
     loads[2].wait()
     loads[3].wait()
@@ -160,137 +135,223 @@
         mine = sb.at[places(g), pl.ds(c * 4, 4)]
         send(mine, mine, c_send.at[2], rc_recv.at[1, g], dc=1)
 
-    def tokens_along_x(d):
-        for s in (1, -1):
-            send(tok.at[rows(d)], tok.at[rows(d)], x_send, x_recv.at[PLACE[d], (1 - s) // 2], dx=s)
+    for s in (1, -1):
+        right_along_z(0, s)
+
+    loads[0].wait()
+    loads[1].wait()
+
+    @pl.loop(0, 14)
+    def _(i):
+        at_tile = pl.ds(pl.multiple_of(i * 128, 128), 128)
+        gate_t[at_tile, :] = gate_v[:, at_tile].T
+        up_t[at_tile, :] = up_v[:, at_tile].T
+
+    def window(dz=0, dy=0):
+        return lax.rem(y + dy + NY, NY) * NZ + lax.rem(z + dz + NZ, NZ)
+
+    def units(dz):
+        return pl.ds(pl.multiple_of(lax.rem(z + dz + NZ, NZ) * F, 32), F)
+
+    upper, lower = pl.ds(0, F), pl.ds(F, F)
+
+    def exchange_weights(d):
+        send(gate_t.at[units(d)], wb.at[dp, upper], w_send, w_recv.at[PLACE[-d], 0], dz=d)
+        send(up_t.at[units(d)], wb.at[dp, lower], w_send, w_recv.at[PLACE[-d], 1], dz=d)
+
+    def order(s):
+        return (0, 1) if s == 1 else (1, 0)
+
+    parts = (upper, lower)
+    for s in (1, -1):
+        for i in order(s):
+            piece = (gate_t, up_t)[i].at[units(0)]
+            send(piece, wb.at[dp, parts[i]], y_send, y_recv.at[0, (1 - s) // 2, i], dy=s)
+    for d in (1, -1):
+        exchange_weights(d)
+    wb[dp, upper, :] = gate_t[units(0), :]
+    wb[dp, lower, :] = up_t[units(0), :]
+
+    def tokens_along_x(d, i):
+        piece = tok.at[rows(d), half[i]]
+        for s in (1, -1):
+            send(piece, piece, x_send, x_recv.at[PLACE[d], (1 - s) // 2, i], dx=s)
+
+    def to_core(d, dx):
+        piece = tok.at[rows(d, dx)]
+        send(piece, piece, c_send.at[0], c_recv.at[PLACE[d]], dc=1)
 
     def pass_tokens(d):
         for s in (1, -1):
             i = (1 - s) // 2
-            wait(tok.at[rows(d)], x_recv.at[PLACE[d], i])
+            wait(tok.at[rows(d), half[i]], x_recv.at[PLACE[d], i, i])
             piece = tok.at[rows(d, -s), half[i]]
             send(piece, piece, x_send, xh_recv.at[PLACE[d], i], dx=s)
+        for s in (1, -1):
+            i = (1 - s) // 2
+            wait(tok.at[rows(d), half[i]], x_recv.at[PLACE[d], i, 1 - i])
+            to_core(d, -s)
 
     def swap_cores(d):
-        place = PLACE[d]
         for i in range(2):
-            wait(tok.at[rows(d), half[i]], xh_recv.at[place, i])
-        mine = tok.at[pl.ds(pl.multiple_of(place * 128 + c * 64, 16), 64)]
-        send(mine, mine, c_send.at[0], c_recv.at[place], dc=1)
-
-    def weights_along_y(d):
-        piece = wb.at[window(d)]
-        for s in (1, -1):
-            send(piece, piece, y_send, y_recv.at[PLACE[d], (1 - s) // 2], dy=s)
+            wait(tok.at[rows(d), half[i]], xh_recv.at[PLACE[d], i])
+        to_core(d, 2)
+
+    def weights_along_y(d, i):
+        piece = wb.at[window(d), parts[i]]
+        for s in (1, -1):
+            send(piece, piece, y_send, y_recv.at[PLACE[d], (1 - s) // 2, i], dy=s)
 
     def pass_weights(d):
         for s in (1, -1):
             i = (1 - s) // 2
-            wait(wb.at[dp], y_recv.at[PLACE[d], i])
-            piece = wb.at[window(d, -s), (upper, lower)[i]]
+            wait(wb.at[dp, upper], y_recv.at[PLACE[d], i, i])
+            piece = wb.at[window(d, -s), parts[i]]
             send(piece, piece, y_send, yh_recv.at[PLACE[d], i], dy=s)
 
-    for s in (1, -1):
-        right_along_z(0, s)
+    def alone(group):
+        return isinstance(group, int) and group in (0, 4)
+
+    def token_span(group):
+        if alone(group):
+            return pl.ds(7 * 128 * (group // 4), 128)
+        return pl.ds(pl.multiple_of(256 * group - 128, 128), 256)
+
+    def spread_documents():
+        loads[5].wait()
+        columns = lax.broadcasted_iota(jnp.int32, (256, 256), 0)
+        placing = (columns == slot_v[...]).astype(jnp.float32).astype(jnp.bfloat16)
+        docs = lax.broadcasted_iota(jnp.int32, (256, 128), 0)
+        for place in range(NZ):
+            one_hot = (docs == idb[place]).astype(jnp.float32).astype(jnp.bfloat16)
+            spread[:, pl.ds(place * 128, 128)] = jnp.dot(
+                placing, one_hot, preferred_element_type=jnp.float32
+            ).astype(jnp.bfloat16)
+
+    def multiply(pair, first, count):
+        blocks = [lax.rem(z + distance + NZ, NZ) for distance in (pair, -1 - pair)]
+        blocks = [i * NZ + block for block in blocks for i in range(NY)]
+        span = pl.ds(first, count)
+        weights = jnp.concatenate([wb[block] for block in blocks], axis=1)
+        lanes = [pl.ds(pl.multiple_of(block * 128, 128), 128) for block in blocks]
+        inputs = jnp.concatenate([tok[span, lane] for lane in lanes], axis=1)
+        acc[:, span] += lax.dot_general(weights, inputs, NT, preferred_element_type=jnp.float32)
+
+    def await_tokens(g):
+        for d in group(g):
+            wait(tok.at[pl.ds(0, 64)], c_recv.at[PLACE[d]])
+
+    def await_weights(g):
+        for d in group(g):
+            for i in range(2):
+                wait(wb.at[dp, upper], y_recv.at[PLACE[d], i, 1 - i])
+                wait(wb.at[dp, upper], yh_recv.at[PLACE[d], i])
+
+    def finish(group):
+        span = token_span(group)
+        first_place = 7 * (group // 4) if alone(group) else 2 * group - 1
+        count = 1 if alone(group) else 2
+        gates = acc[:F, span]
+        act[pl.ds(first, F), span] = (gates / (1.0 + jnp.exp(-gates)) * acc[F:, span]).astype(jnp.bfloat16)
+        left = jnp.dot(ql_v[...], act[:, span], preferred_element_type=jnp.float32)
+        for q in range(16):
+            hidden = q // 2
+            at_row = hidden % 2 * 256 + hidden // 2 * 64 + q % 2 * R
+            right = [
+                rb[first_place + i, at_row:at_row + R].astype(jnp.int32).astype(jnp.float32)
+                * sb[first_place + i, hidden % 2 * 4 + hidden // 2]
+                for i in range(count)
+            ]
+            right = right[0] if count == 1 else jnp.concatenate(right, axis=1)
+            scores[q:q + 1, span] = jnp.sum(
+                left[q * R:(q + 1) * R] * right, axis=0, keepdims=True
+            )
+
     right_along_x(0)
-    for g in range(1, 7):
+    acc[...] = jnp.zeros_like(acc)
+    act[...] = jnp.zeros_like(act)
+    scores[...] = jnp.zeros_like(scores)
+    first = pl.multiple_of(F * z - (5 * z) // 3 * 128, 32)
+    for g in range(1, 5):
         if g < 4:
+            for i in range(2):
+                for d in group(g):
+                    s = 1 if d < 0 else -1
+                    place = PLACE[d]
+                    wait(tok.at[rows(d), half[i]], z_recv.at[place, i])
+                    if g < 3 or s == 1 - 2 * i:
+                        piece = tok.at[rows(d), half[i]]
+                        send(piece, tok.at[rows(d - s), half[i]], z_send, z_recv.at[PLACE[d - s], i], dz=s)
+                    tokens_along_x(d, i)
+        else:
+            for i in range(2):
+                wait(tok.at[rows(4), half[i]], z_recv.at[PLACE[4], i])
+                tokens_along_x(4, i)
+        for d in group(g):
+            to_core(d, 0)
+        for d in group(g):
+            for i in range(3):
+                wait((rb.at[0, k_rows()], sb.at[0, scale_row()], idb.at[0])[i], rz_recv.at[i, PLACE[d]])
+            s = 1 if d < 0 else -1
+            if g < 3 or d == -3:
+                right_along_z(d, s)
+        right_along_x(g)
+        for d in group(g + 1) if g < 4 else ():
+            exchange_weights(d)
+        if g > 1:
+            for d in group(g - 1):
+                pass_tokens(d)
+            pass_right(g - 1)
+        if g > 2:
+            for d in group(g - 2):
+                swap_cores(d)
+            swap_right(g - 2)
+        for d in group(g - 1):
+            pass_weights(d)
+        if g == 1:
+            pass_right(0)
+        if g == 3:
+            loads[7].wait()
+            await_weights(0)
+            await_weights(1)
+            await_tokens(1)
+            multiply(0, 0, 384)
+        if g == 4:
+            spread_documents()
+            await_weights(2)
+            multiply(1, 0, 384)
+        for i in range(2):
             for d in group(g):
-                s = 1 if d < 0 else -1
-                place = PLACE[d]
-                wait(tok.at[rows(d)], z_recv.at[place])
-                if g < 3:
-                    send(tok.at[rows(d)], tok.at[rows(d - s)], z_send, z_recv.at[PLACE[d - s]], dz=s)
-                else:
-                    i = (1 - s) // 2
-                    send(
-                        tok.at[rows(d), half[i]], tok.at[rows(4), half[i]], z_send,
-                        z_recv.at[NZ - 1 + i], dz=s,
-                    )
-                tokens_along_x(d)
-            for d in group(g + 1):
-                exchange_weights(d)
-        if g == 4:
-            for i in range(2):
-                wait(tok.at[rows(4), half[i]], z_recv.at[NZ - 1 + i])
-            tokens_along_x(4)
-        if g <= 4:
-            for d in group(g):
-                for i in range(3):
-                    wait((rb.at[0, k_rows()], sb.at[0, scale_row()], idb.at[0])[i], rz_recv.at[i, PLACE[d]])
-                s = 1 if d < 0 else -1
-                if g < 3 or d == -3:
-                    right_along_z(d, s)
-            right_along_x(g)
-            for d in group(g):
-                wait(wb.at[dp], w_recv.at[PLACE[d]])
-                weights_along_y(d)
-        h = g - 1
-        if h <= 4:
-            for d in group(h):
-                pass_weights(d)
-                if h > 0:
-                    pass_tokens(d)
-            pass_right(h)
-        h = g - 2
-        if 0 <= h <= 4:
-            if h > 0:
-                for d in group(h):
-                    swap_cores(d)
-            swap_right(h)
-
-    loads[5].wait()
-    columns = lax.broadcasted_iota(jnp.int32, (256, 256), 0)
-    placing = (columns == slot_v[...]).astype(jnp.float32).astype(jnp.bfloat16)
-    docs = lax.broadcasted_iota(jnp.int32, (256, 128), 0)
-    for place in range(NZ):
-        one_hot = (docs == idb[place]).astype(jnp.float32).astype(jnp.bfloat16)
-        spread[:, pl.ds(place * 128, 128)] = jnp.dot(
-            placing, one_hot, preferred_element_type=jnp.float32
-        ).astype(jnp.bfloat16)
-
-    for d in DIST:
-        for i in range(2):
-            wait(wb.at[dp, upper], yh_recv.at[PLACE[d], i])
-        if d != 0:
-            wait(tok.at[pl.ds(0, 64)], c_recv.at[PLACE[d]])
+                wait(wb.at[dp, upper], w_recv.at[PLACE[d], i])
+                weights_along_y(d, i)
+        if g == 2:
+            swap_right(0)
+    pass_tokens(4)
+    pass_right(4)
+    for d in group(3):
+        swap_cores(d)
+    swap_right(3)
+    await_tokens(2)
+    pl.loop(0, 2)(lambda pair: multiply(pair, 384, 256))
+    pass_weights(4)
+    swap_cores(4)
+    swap_right(4)
+    await_weights(3)
+    multiply(2, 0, 640)
+    await_tokens(3)
+    pl.loop(0, 3)(lambda pair: multiply(pair, 640, 256))
     for g in range(5):
         wait(rb.at[places(g), pl.ds(0, 256)], rc_recv.at[0, g])
         wait(sb.at[places(g), pl.ds(0, 4)], rc_recv.at[1, g])
     loads[6].wait()
-    loads[7].wait()
-    act[...] = jnp.zeros_like(act)
-    scores[...] = jnp.zeros_like(scores)
-    first = pl.multiple_of(F * z - (5 * z) // 3 * 128, 32)
-
-    @pl.loop(0, 4)
-    def _(j):
-        span = pl.ds(pl.multiple_of(j * 256, 256), 256)
-        acc[...] = jnp.zeros_like(acc)
-
-        @pl.loop(0, 4)
-        def _(k):
-            weights = jnp.concatenate([wb[k * 8 + i] for i in range(8)], axis=1)
-            inputs = tok[span, pl.ds(pl.multiple_of(k * 1024, 1024), 1024)]
-            acc[...] += lax.dot_general(weights, inputs, NT, preferred_element_type=jnp.float32)
-
-        gates = acc[:F]
-        act[pl.ds(first, F), :] = (gates / (1.0 + jnp.exp(-gates)) * acc[F:]).astype(jnp.bfloat16)
-        left = jnp.dot(ql_v[...], act[...], preferred_element_type=jnp.float32)
-        for q in range(16):
-            hidden = q // 2
-            at_row = hidden % 2 * 256 + hidden // 2 * 64 + q % 2 * R
-            right = jnp.concatenate(
-                [
-                    rb[2 * j + i, at_row:at_row + R].astype(jnp.int32).astype(jnp.float32)
-                    * sb[2 * j + i, hidden % 2 * 4 + hidden // 2]
-                    for i in range(2)
-                ],
-                axis=1,
-            )
-            scores[q:q + 1, span] = jnp.sum(
-                left[q * R:(q + 1) * R] * right, axis=0, keepdims=True
-            )
+    await_weights(4)
+    multiply(3, 0, 896)
+    finish(0)
+    pl.loop(1, 4)(finish)
+    await_tokens(4)
+    weights = jnp.concatenate([wb[i] for i in range(NY * NZ)], axis=1)
+    acc[:, 896:] = lax.dot_general(weights, tok[896:, :], NT, preferred_element_type=jnp.float32)
+    finish(4)
 
     rest = scores[...]
     columns_sum = jnp.zeros((256, 128), jnp.float32)
@@ -368,8 +429,8 @@
             pltpu.VMEM((512, 384), bf16),
             pltpu.VMEM((1, 128), i32),
             pltpu.VMEM((1, 256), i32),
-            pltpu.VMEM((2 * F, 256), f32),
-            pltpu.VMEM((384, 256), bf16),
+            pltpu.VMEM((2 * F, 1024), f32),
+            pltpu.VMEM((384, 1024), bf16),
             pltpu.VMEM((128, 1024), f32),
             pltpu.VMEM((256, 1024), bf16),
             pltpu.VMEM((32, 8, 128), f32),
@@ -377,7 +438,7 @@
             pltpu.VMEM((8, 128), f32),
             pltpu.VMEM((8, 8, 128), f32),
             dma((8,)), dma, dma, dma((3,)), dma, dma, dma((7,)), dma((2,)),
-            dma((9,)), dma((8, 2)), dma((8, 2)), dma((8,)), dma((8,)), dma((8, 2)), dma((8, 2)),
+            dma((8, 2)), dma((8, 2, 2)), dma((8, 2)), dma((8,)), dma((8, 2)), dma((8, 2, 2)), dma((8, 2)),
             dma((3, 8)), dma((2, 5, 2)), dma((3, 5)), dma((2, 5)), dma((2,)),
         ],
         compiler_params=pltpu.CompilerParams(

time: 78.6 us -> 73.5 us (0.935)
  Pallas kernels: 77.3 us -> 72.1 us
    pallas_call x1, Pallas kernels: 77.3 us -> 72.1 us  [local(): pl.pallas_call(kernel, out_shape=jax.ShapeDtypeStruct((2, 8), f32), in_sp...]
where the time goes in v4:
time: 73.5 us; the launch traced here: 73.4 us
  Pallas kernels  72.1 us (98%)
  local copies, waits for them, and re-layouts  1.24 us (2%)
    pallas_call x1, Pallas kernels, local(): pl.pallas_call(kernel, out_shape=jax.ShapeDtypeStruct((2, 8), f32), in_sp...  72.1 us

profile of v4, /device:TPU:1, one launch (start us, length us, event | category | flops | bytes accessed | tf_op | source)
XLA Modules:
  0.0 73.4 jit_solution(17105077786809265907)
XLA Ops:
  0.0 72.1 %influence.1 = f32[2,8]{1,0:T(2,128)} custom-call(bf16[128,4096]{1,0:T(8,128)(2,1)} %tokens.1, bf16[128,1792]{1,0:T(8,128)(2,1)} %gate.1, bf16[128,1792]{1,0:T(8,128)(2,1)} %up.1, bf16[128,4096]{1,0:T(8,128)(2,1)} %cot.1, bf16[512,1792]{1,0:T(8,128)(2,1)} %ql.1, bf16[64,4096]{1,0:T(8,128)(2,1)} %qr.1, s32[1,128]{1,0:T(1,128)} %bitcast.3, s32[1,256]{1,0:T(1,128)} %bitcast.2), custom_call_target="tpu_custom_call" | custom-call | tf_op jit(solution)/shard_map/influence/pallas_call | solution.py:412
  72.1 1.2 %copy.10 = f32[2,8]{1,0:T(2,128)} copy(f32[2,8]{1,0:T(2,128)} %influence.1) | data formatting | bytes 128

commit v5 on v4

--- a/solution.py
+++ b/solution.py
@@ -209,17 +209,10 @@
             piece = wb.at[window(d, -s), parts[i]]
             send(piece, piece, y_send, yh_recv.at[PLACE[d], i], dy=s)
 
-    def alone(group):
-        return isinstance(group, int) and group in (0, 4)
-
-    def token_span(group):
-        if alone(group):
-            return pl.ds(7 * 128 * (group // 4), 128)
-        return pl.ds(pl.multiple_of(256 * group - 128, 128), 256)
-
     def spread_documents():
         loads[5].wait()
-        columns = lax.broadcasted_iota(jnp.int32, (256, 256), 0)
+        row = lax.broadcasted_iota(jnp.int32, (256, 256), 0)
+        columns = (row & 31) * 8 + lax.shift_right_logical(row, 5)
         placing = (columns == slot_v[...]).astype(jnp.float32).astype(jnp.bfloat16)
         docs = lax.broadcasted_iota(jnp.int32, (256, 128), 0)
         for place in range(NZ):
@@ -228,14 +221,15 @@
                 placing, one_hot, preferred_element_type=jnp.float32
             ).astype(jnp.bfloat16)
 
-    def multiply(pair, first, count):
-        blocks = [lax.rem(z + distance + NZ, NZ) for distance in (pair, -1 - pair)]
+    def multiply(taken, first, count):
+        blocks = [lax.rem(z + DIST[place] + NZ, NZ) for place in taken]
         blocks = [i * NZ + block for block in blocks for i in range(NY)]
         span = pl.ds(first, count)
         weights = jnp.concatenate([wb[block] for block in blocks], axis=1)
         lanes = [pl.ds(pl.multiple_of(block * 128, 128), 128) for block in blocks]
         inputs = jnp.concatenate([tok[span, lane] for lane in lanes], axis=1)
-        acc[:, span] += lax.dot_general(weights, inputs, NT, preferred_element_type=jnp.float32)
+        product = lax.dot_general(weights, inputs, NT, preferred_element_type=jnp.float32)
+        acc[:, span] = product if 0 in taken else acc[:, span] + product
 
     def await_tokens(g):
         for d in group(g):
@@ -247,10 +241,8 @@
                 wait(wb.at[dp, upper], y_recv.at[PLACE[d], i, 1 - i])
                 wait(wb.at[dp, upper], yh_recv.at[PLACE[d], i])
 
-    def finish(group):
-        span = token_span(group)
-        first_place = 7 * (group // 4) if alone(group) else 2 * group - 1
-        count = 1 if alone(group) else 2
+    def finish(j):
+        span = pl.ds(j * 256, 256)
         gates = acc[:F, span]
         act[pl.ds(first, F), span] = (gates / (1.0 + jnp.exp(-gates)) * acc[F:, span]).astype(jnp.bfloat16)
         left = jnp.dot(ql_v[...], act[:, span], preferred_element_type=jnp.float32)
@@ -258,17 +250,15 @@
             hidden = q // 2
             at_row = hidden % 2 * 256 + hidden // 2 * 64 + q % 2 * R
             right = [
-                rb[first_place + i, at_row:at_row + R].astype(jnp.int32).astype(jnp.float32)
-                * sb[first_place + i, hidden % 2 * 4 + hidden // 2]
-                for i in range(count)
+                rb[2 * j + i, at_row:at_row + R].astype(jnp.int32).astype(jnp.float32)
+                * sb[2 * j + i, hidden % 2 * 4 + hidden // 2]
+                for i in range(2)
             ]
-            right = right[0] if count == 1 else jnp.concatenate(right, axis=1)
             scores[q:q + 1, span] = jnp.sum(
-                left[q * R:(q + 1) * R] * right, axis=0, keepdims=True
+                left[q * R:(q + 1) * R] * jnp.concatenate(right, axis=1), axis=0, keepdims=True
             )
 
     right_along_x(0)
-    acc[...] = jnp.zeros_like(acc)
     act[...] = jnp.zeros_like(act)
     scores[...] = jnp.zeros_like(scores)
     first = pl.multiple_of(F * z - (5 * z) // 3 * 128, 32)
@@ -302,56 +292,51 @@
             for d in group(g - 1):
                 pass_tokens(d)
             pass_right(g - 1)
-        if g > 2:
-            for d in group(g - 2):
-                swap_cores(d)
-            swap_right(g - 2)
-        for d in group(g - 1):
-            pass_weights(d)
-        if g == 1:
-            pass_right(0)
         if g == 3:
             loads[7].wait()
             await_weights(0)
             await_weights(1)
             await_tokens(1)
-            multiply(0, 0, 384)
+            multiply((0, 1, 2), 0, 384)
         if g == 4:
             spread_documents()
             await_weights(2)
-            multiply(1, 0, 384)
+            await_tokens(2)
+            multiply((0, 1, 2), 384, 256)
+            multiply((3, 4), 0, 640)
+        for d in group(g - 1):
+            pass_weights(d)
+        if g == 1:
+            pass_right(0)
         for i in range(2):
             for d in group(g):
                 wait(wb.at[dp, upper], w_recv.at[PLACE[d], i])
                 weights_along_y(d, i)
-        if g == 2:
-            swap_right(0)
+        if g > 1:
+            for d in group(g - 1):
+                swap_cores(d)
+        if g > 1:
+            swap_right(g - 2)
     pass_tokens(4)
     pass_right(4)
-    for d in group(3):
-        swap_cores(d)
     swap_right(3)
-    await_tokens(2)
-    pl.loop(0, 2)(lambda pair: multiply(pair, 384, 256))
+    await_weights(3)
+    multiply((5, 6), 0, 640)
     pass_weights(4)
+    await_tokens(3)
+    multiply((0, 1, 2, 3, 4, 5, 6), 640, 256)
     swap_cores(4)
     swap_right(4)
-    await_weights(3)
-    multiply(2, 0, 640)
-    await_tokens(3)
-    pl.loop(0, 3)(lambda pair: multiply(pair, 640, 256))
     for g in range(5):
         wait(rb.at[places(g), pl.ds(0, 256)], rc_recv.at[0, g])
         wait(sb.at[places(g), pl.ds(0, 4)], rc_recv.at[1, g])
     loads[6].wait()
+    await_tokens(4)
+    multiply((0, 1, 2, 3, 4, 5, 6), 896, 128)
     await_weights(4)
-    multiply(3, 0, 896)
-    finish(0)
-    pl.loop(1, 4)(finish)
-    await_tokens(4)
-    weights = jnp.concatenate([wb[i] for i in range(NY * NZ)], axis=1)
-    acc[:, 896:] = lax.dot_general(weights, tok[896:, :], NT, preferred_element_type=jnp.float32)
-    finish(4)
+    multiply((7,), 0, 1024)
+    for j in range(4):
+        finish(j)
 
     rest = scores[...]
     columns_sum = jnp.zeros((256, 128), jnp.float32)
@@ -359,31 +344,32 @@
         rounded = rest.astype(jnp.bfloat16)
         rest = rest - rounded.astype(jnp.float32)
         columns_sum += lax.dot_general(spread[...], rounded, NT, preferred_element_type=jnp.float32)
-    part[...] = columns_sum.reshape(32, 8, 128)
-
-    @pl.loop(1, 32)
-    def _(k):
-        to = lax.rem(dp + k, 32)
-        pltpu.make_async_remote_copy(
-            part.at[to], got.at[dp], tail_send.at[0], tail_recv.at[0],
-            device_id=(to, hid), device_id_type=MESH,
-        ).start()
-
+    packed = columns_sum[:32]
+    for j in range(1, 8):
+        packed += pltpu.roll(columns_sum[j * 32:(j + 1) * 32], j * 16, 1)
+    for k in range(32):
+        part[k] = packed[k:k + 1]
+
+    def hops(dy, dz):
+        return min(dy, NY - dy) + min(dz, NZ - dz)
+
+    offsets = [(dy, dz) for dy in range(NY) for dz in range(NZ) if dy + dz]
+    for dy, dz in sorted(offsets, key=lambda o: -hops(*o)):
+        send(part.at[window(dz, dy)], got.at[dp], tail_send.at[0], tail_recv.at[0], dy=dy, dz=dz)
     wait(got.at[pl.ds(0, 31)], tail_recv.at[0])
     got[dp] = part[dp]
     tile[...] = jnp.sum(got[...], axis=0)
-    for k in range(1, hidden_count):
-        pltpu.make_async_remote_copy(
-            tile, tiles.at[hid], tail_send.at[1], tail_recv.at[1],
-            device_id=(dp, lax.rem(hid + k, hidden_count)), device_id_type=MESH,
-        ).start()
+    for dx, dc in ((2, 1), (2, 0), (1, 1), (3, 1), (1, 0), (3, 0), (0, 1)):
+        send(tile, tiles.at[hid], tail_send.at[1], tail_recv.at[1], dx=dx, dc=dc)
     wait(tiles.at[pl.ds(0, hidden_count - 1)], tail_recv.at[1])
     tiles[hid] = tile[...]
     total = jnp.sum(tiles[...], axis=0)
-    query = lax.broadcasted_iota(jnp.int32, (8, 128), 0) + 2 * hid
-    pick = (lax.broadcasted_iota(jnp.int32, (8, 128), 1) == query).astype(jnp.float32)
+    lane = lax.broadcasted_iota(jnp.int32, (8, 128), 1)
+    row = lax.broadcasted_iota(jnp.int32, (8, 128), 0)
+    mine = jnp.where((lane & 15) == row + 2 * hid, jnp.broadcast_to(total, (8, 128)), 0.0)
+    pick = (lax.shift_right_logical(lane, 4) == row).astype(jnp.float32)
     result = lax.dot_general(
-        pick, total, NT, precision=lax.Precision.HIGHEST, preferred_element_type=jnp.float32
+        mine, pick, NT, precision=lax.Precision.HIGHEST, preferred_element_type=jnp.float32
     )
     out[...] = result[:2]
 
@@ -433,10 +419,10 @@
             pltpu.VMEM((384, 1024), bf16),
             pltpu.VMEM((128, 1024), f32),
             pltpu.VMEM((256, 1024), bf16),
-            pltpu.VMEM((32, 8, 128), f32),
-            pltpu.VMEM((32, 8, 128), f32),
-            pltpu.VMEM((8, 128), f32),
-            pltpu.VMEM((8, 8, 128), f32),
+            pltpu.VMEM((32, 1, 128), f32),
+            pltpu.VMEM((32, 1, 128), f32),
+            pltpu.VMEM((1, 128), f32),
+            pltpu.VMEM((8, 1, 128), f32),
             dma((8,)), dma, dma, dma((3,)), dma, dma, dma((7,)), dma((2,)),
             dma((8, 2)), dma((8, 2, 2)), dma((8, 2)), dma((8,)), dma((8, 2)), dma((8, 2, 2)), dma((8, 2)),
             dma((3, 8)), dma((2, 5, 2)), dma((3, 5)), dma((2, 5)), dma((2,)),

time: 73.5 us -> 71 us (0.966)
  Pallas kernels: 72.1 us -> 69.7 us
    pallas_call x1, Pallas kernels: 72.1 us -> 69.7 us  [local(): pl.pallas_call(kernel, out_shape=jax.ShapeDtypeStruct((2, 8), f32), in_sp...]
where the time goes in v5:
time: 71 us
  Pallas kernels  69.7 us (98%)
  local copies, waits for them, and re-layouts  1.24 us (2%)
    pallas_call x1, Pallas kernels, local(): pl.pallas_call(kernel, out_shape=jax.ShapeDtypeStruct((2, 8), f32), in_sp...  69.7 us

profile of v5, /device:TPU:1, one launch (start us, length us, event | category | flops | bytes accessed | tf_op | source)
XLA Modules:
  0.0 71.0 jit_solution(5863075540991666060)
XLA Ops:
  0.0 69.7 %influence.1 = f32[2,8]{1,0:T(2,128)} custom-call(bf16[128,4096]{1,0:T(8,128)(2,1)} %tokens.1, bf16[128,1792]{1,0:T(8,128)(2,1)} %gate.1, bf16[128,1792]{1,0:T(8,128)(2,1)} %up.1, bf16[128,4096]{1,0:T(8,128)(2,1)} %cot.1, bf16[512,1792]{1,0:T(8,128)(2,1)} %ql.1, bf16[64,4096]{1,0:T(8,128)(2,1)} %qr.1, s32[1,128]{1,0:T(1,128)} %bitcast.3, s32[1,256]{1,0:T(1,128)} %bitcast.2), custom_call_target="tpu_custom_call" | custom-call | tf_op jit(solution)/shard_map/influence/pallas_call | solution.py:398
  69.7 1.2 %copy.10 = f32[2,8]{1,0:T(2,128)} copy(f32[2,8]{1,0:T(2,128)} %influence.1) | data formatting | bytes 128

commit v6 on v5

--- a/solution.py
+++ b/solution.py
@@ -260,7 +260,6 @@
 
     right_along_x(0)
     act[...] = jnp.zeros_like(act)
-    scores[...] = jnp.zeros_like(scores)
     first = pl.multiple_of(F * z - (5 * z) // 3 * 128, 32)
     for g in range(1, 5):
         if g < 4:
@@ -338,12 +337,18 @@
     for j in range(4):
         finish(j)
 
-    rest = scores[...]
-    columns_sum = jnp.zeros((256, 128), jnp.float32)
+    rest = scores[:16]
+    rounded = []
     for _ in range(3):
-        rounded = rest.astype(jnp.bfloat16)
-        rest = rest - rounded.astype(jnp.float32)
-        columns_sum += lax.dot_general(spread[...], rounded, NT, preferred_element_type=jnp.float32)
+        rounded.append(rest.astype(jnp.bfloat16))
+        rest = rest - rounded[-1].astype(jnp.float32)
+    rounded.append(jnp.zeros((80, 1024), jnp.bfloat16))
+    columns_sum = lax.dot_general(
+        spread[...], jnp.concatenate(rounded, axis=0), NT, preferred_element_type=jnp.float32
+    )
+    lane = lax.broadcasted_iota(jnp.int32, (256, 128), 1)
+    columns_sum += pltpu.roll(columns_sum, 112, 1) + pltpu.roll(columns_sum, 96, 1)
+    columns_sum = jnp.where(lane < 16, columns_sum, 0.0)
     packed = columns_sum[:32]
     for j in range(1, 8):
         packed += pltpu.roll(columns_sum[j * 32:(j + 1) * 32], j * 16, 1)
@@ -417,7 +422,7 @@
             pltpu.VMEM((1, 256), i32),
             pltpu.VMEM((2 * F, 1024), f32),
             pltpu.VMEM((384, 1024), bf16),
-            pltpu.VMEM((128, 1024), f32),
+            pltpu.VMEM((16, 1024), f32),
             pltpu.VMEM((256, 1024), bf16),
             pltpu.VMEM((32, 1, 128), f32),
             pltpu.VMEM((32, 1, 128), f32),

time: 71 us -> 70.4 us (level)
  no operation moved by 1% of the time
where the time goes in v6:
time: 70.4 us; the launch traced here: 70.3 us
  Pallas kernels  69 us (98%)
  local copies, waits for them, and re-layouts  1.24 us (2%)
    pallas_call x1, Pallas kernels, local(): pl.pallas_call(kernel, out_shape=jax.ShapeDtypeStruct((2, 8), f32), in_sp...  69 us

profile of v6, /device:TPU:1, one launch (start us, length us, event | category | flops | bytes accessed | tf_op | source)
XLA Modules:
  0.0 70.3 jit_solution(6410088994299423610)
XLA Ops:
  0.0 69.0 %influence.1 = f32[2,8]{1,0:T(2,128)} custom-call(bf16[128,4096]{1,0:T(8,128)(2,1)} %tokens.1, bf16[128,1792]{1,0:T(8,128)(2,1)} %gate.1, bf16[128,1792]{1,0:T(8,128)(2,1)} %up.1, bf16[128,4096]{1,0:T(8,128)(2,1)} %cot.1, bf16[512,1792]{1,0:T(8,128)(2,1)} %ql.1, bf16[64,4096]{1,0:T(8,128)(2,1)} %qr.1, s32[1,128]{1,0:T(1,128)} %bitcast.3, s32[1,256]{1,0:T(1,128)} %bitcast.2), custom_call_target="tpu_custom_call" | custom-call | tf_op jit(solution)/shard_map/influence/pallas_call | solution.py:403
  69.0 1.2 %copy.10 = f32[2,8]{1,0:T(2,128)} copy(f32[2,8]{1,0:T(2,128)} %influence.1) | data formatting | bytes 128
